TPU v7x, 512 devices: a whole 4x8x8 slice. The times are simulated.
512 devices in a mesh: section: 16 (over y, core), dp: 16 (over x, z_hi), mp: 2 (over z_lo).
Axes of the slice: x: 4, y: 8, z: 8 (z_hi: 4, z_lo: 2; z = z_hi * 2 + z_lo), core: 2. Of those that a mesh axis runs over, the one named last changes fastest.
Arguments:
- section_in: bfloat16 [16, 16, 104, 7168], P('section', 'dp', None, 'mp'), may hold values from -6 to 6
- vision_rows: bfloat16 [16, 24, 7168], P('dp', None, 'mp'), may hold values from -6 to 6
- alternate: int32 [16, 104], P('dp'), may hold values from -1 to 23, as said below
- grad_in: bfloat16 [16, 16, 104, 7168], P('section', 'dp', None, 'mp'), may hold values from -1.5 to 1.5
- parked: bfloat16 [16, 16, 104, 7168], P('section', 'dp', None, 'mp'), may hold values from -6 to 6
- w_down: bfloat16 [16, 256, 7168], P('section', 'dp', 'mp'), may hold values from -0.0625 to 0.0625
- w_up: bfloat16 [16, 256, 7168], P('section', 'dp', 'mp'), may hold values from -0.375 to 0.375
Outputs:
- section_out: bfloat16 [16, 16, 104, 7168], P('section', 'dp', None, 'mp')
- parked_out: bfloat16 [16, 16, 104, 7168], P('section', 'dp', None, 'mp')
- input_grad: bfloat16 [16, 16, 104, 7168], P('section', 'dp', None, 'mp')
- up_grad: bfloat16 [16, 256, 7168], P('section', 'dp', 'mp')
- down_grad: bfloat16 [16, 256, 7168], P('section', 'dp', 'mp')
Inputs may be any that keep to these rules, and one draw needn't show every extreme that they name: `alternate`: in each replica every image-token row 0 to 23 fills exactly one row, in increasing order along the rows; all other entries are -1.
All inputs are finite; a program needn't handle non-finite values.
Results may differ from a plain program's by a relative error of at most 0.019.
Values may be sent and summed in bfloat16 or wider, within the bound.
A program may use at most 64 MiB of HBM per device.

v0:
```python
import jax
import jax.numpy as jnp
from jax import lax
from jax.sharding import PartitionSpec as P


def partner(value, axis, apart):
    mask = 2**apart
    pairs = [(source, source ^ mask) for source in range(lax.axis_size(axis))]
    return lax.ppermute(value, axis, pairs)


def passed_along(value, axis, steps):
    count = lax.axis_size(axis)
    pairs = [(source, (source + steps) % count) for source in range(count)]
    return lax.ppermute(value, axis, pairs)


def gelu_slope(values, upstream):
    return jax.vjp(lambda inner: jax.nn.gelu(inner, approximate=True), values)[1](upstream)[0]


def mirrored(stacked):
    levels = lax.axis_size("section").bit_length() - 1
    for bit_index in range(levels):
        stacked = partner(stacked, "section", bit_index)
    return stacked


def local(section_in, vision_rows, alternate, grad_in, parked, w_down, w_up):
    down_full, up_full = (
        lax.all_gather(w_down[0], "dp", axis=0, tiled=True),
        lax.all_gather(w_up[0], "dp", axis=0, tiled=True),
    )
    picks = alternate[0]
    chosen = jnp.take(vision_rows[0], jnp.maximum(picks, 0), axis=0)
    leading = lax.axis_index("section") == 0
    forward_in = jnp.where(jnp.logical_and(picks >= 0, leading)[:, None], chosen, section_in[0, 0])
    moved = mirrored(jnp.stack([forward_in, parked[0, 0]]))
    backward_in = moved[1]
    upstream = grad_in[0, 0]
    by_width = (((1,), (1,)), ((), ()))
    by_rows = (((0,), (0,)), ((), ()))
    fwd_part = lax.dot_general(forward_in, down_full, by_width, preferred_element_type=jnp.float32)
    bwd_part = lax.dot_general(backward_in, down_full, by_width, preferred_element_type=jnp.float32)
    slope_part = lax.dot_general(upstream, up_full, by_width, preferred_element_type=jnp.float32)
    fwd_pre, bwd_pre, slope_pre = lax.psum((fwd_part, bwd_part, slope_part), "mp")
    fwd_act = jax.nn.gelu(fwd_pre, approximate=True).astype(jnp.bfloat16)
    outputs = (
        forward_in.astype(jnp.float32)
        + jnp.dot(fwd_act, up_full, preferred_element_type=jnp.float32)
    ).astype(jnp.bfloat16)
    received = passed_along(outputs, "section", 1)
    bwd_act = jax.nn.gelu(bwd_pre, approximate=True).astype(jnp.bfloat16)
    pre_grad = gelu_slope(bwd_pre, slope_pre).astype(jnp.bfloat16)
    input_grad = (
        upstream.astype(jnp.float32)
        + jnp.dot(pre_grad, down_full, preferred_element_type=jnp.float32)
    ).astype(jnp.bfloat16)
    up_term = lax.dot_general(bwd_act, upstream, by_rows, preferred_element_type=jnp.float32)
    down_term = lax.dot_general(pre_grad, backward_in, by_rows, preferred_element_type=jnp.float32)
    up_sum, down_sum = (
        lax.psum_scatter(
            up_term.astype(jnp.bfloat16), "dp", scatter_dimension=0, tiled=True
        ).astype(jnp.float32),
        lax.psum_scatter(
            down_term.astype(jnp.bfloat16), "dp", scatter_dimension=0, tiled=True
        ).astype(jnp.float32),
    )
    factor = 1.0 / lax.axis_size("dp")
    up_grad = (up_sum * factor).astype(jnp.bfloat16)
    down_grad = (down_sum * factor).astype(jnp.bfloat16)
    return (
        received[None, None],
        moved[0][None, None],
        input_grad[None, None],
        up_grad[None],
        down_grad[None],
    )


def solution(mesh):
    placed = (
        P("section", "dp", None, "mp"),
        P("dp", None, "mp"),
        P("dp", None),
        P("section", "dp", None, "mp"),
        P("section", "dp", None, "mp"),
        P("section", "dp", "mp"),
        P("section", "dp", "mp"),
    )
    return jax.shard_map(
        local,
        mesh=mesh,
        in_specs=placed,
        out_specs=(
            P("section", "dp", None, "mp"),
            P("section", "dp", None, "mp"),
            P("section", "dp", None, "mp"),
            P("section", "dp", "mp"),
            P("section", "dp", "mp"),
        ),
        check_vma=False,
    )
```

profile of v0, /device:TPU:6, one launch (start us, length us, event | category | flops | bytes accessed | tf_op | source)
XLA Modules:
  0.0 442.7 jit_solution(2016147720513935312)
XLA Ops:
  7.2 0.0 copy-start
  7.2 0.0 all-gather.7.cloned.1.call-start
  7.2 0.7 all-gather.7.cloned.1.call-update
  7.9 0.0 all-gather.5.cloned.1.call-start
  8.0 0.7 maximum_bitcast_fusion
  8.6 0.7 and_bitcast_fusion
  9.3 0.0 copy-start.7
  9.3 1.0 gather_fusion
  10.3 0.0 copy-start.8
  10.3 0.1 copy-done.7
  10.4 0.2 bitcast_select_fusion
  10.6 0.0 copy-start.4
  10.6 0.8 copy-done.8
  11.5 0.1 pad_maximum_fusion
  11.6 1.9 collective-permute-start.1
  13.5 3.3 collective-permute-done.1
  16.8 3.5 collective-permute-start.2
  20.3 0.0 all-gather.5.cloned.1.call-update
  20.3 0.0 all-reduce.3.cloned.1.call-start
  20.4 33.1 %collective-permute-done.2 = bf16[2,104,3584]{2,1,0:T(8,128)(2,1)} collective-permute-done((bf16[2,104,3584]{2,1,0:T(8,128)(2,1)S(1)}, bf16[2,104,3584]{2,1,0:T(8,128)(2,1)}, u32[]{:S(2)}, u32[]{:S(2)}) %collective-permute-start.2) | collective-permute-done | bytes 1490976 | tf_op jit(solution)/shard_map/ppermute | solution.py:10
  53.5 4.5 %collective-permute-start.3 = (bf16[2,104,3584]{2,1,0:T(8,128)(2,1)}, bf16[2,104,3584]{2,1,0:T(8,128)(2,1)}, u32[]{:S(2)}, u32[]{:S(2)}) collective-permute-start(bf16[2,104,3584]{2,1,0:T(8,128)(2,1)} %collective-permute-done.2), channel_id=1, source_target_pairs={{0,128},{32,160},{64,192},{96,224},{128,0},{160,32},{192,64},{224,... | collective-permute-start | bytes 4472840 | tf_op jit(solution)/shard_map/ppermute | solution.py:10
  58.0 64.4 %collective-permute-done.3 = bf16[2,104,3584]{2,1,0:T(8,128)(2,1)} collective-permute-done((bf16[2,104,3584]{2,1,0:T(8,128)(2,1)}, bf16[2,104,3584]{2,1,0:T(8,128)(2,1)}, u32[]{:S(2)}, u32[]{:S(2)}) %collective-permute-start.3) | collective-permute-done | bytes 1490976 | tf_op jit(solution)/shard_map/ppermute | solution.py:10
  122.4 7.7 %collective-permute-start.4 = (bf16[2,104,3584]{2,1,0:T(8,128)(2,1)}, bf16[2,104,3584]{2,1,0:T(8,128)(2,1)S(1)}, u32[]{:S(2)}, u32[]{:S(2)}) collective-permute-start(bf16[2,104,3584]{2,1,0:T(8,128)(2,1)} %collective-permute-done.3), channel_id=1, source_target_pairs={{0,256},{32,288},{64,320},{96,352},{128,384},{160,416},{192,448},{... | collective-permute-start | bytes 4472840 | tf_op jit(solution)/shard_map/ppermute | solution.py:10
  130.1 0.0 all-gather.7.cloned.1.call-done
  130.1 2.9 fusion.3
  133.0 10.7 %all-gather.5.cloned.1.call-done = bf16[1,256,3584]{2,1,0:T(8,128)(2,1)} async-done(((bf16[1,16,3584]{2,1,0:T(8,128)(2,1)}), bf16[1,256,3584]{2,1,0:T(8,128)(2,1)}) %all-gather.5.cloned.1.call-update) | async-done | bytes 1835024 | tf_op jit(solution)/shard_map/all_gather | solution.py:32
  143.8 3.2 fusion.9
  147.0 48.5 %collective-permute-done.4 = bf16[2,104,3584]{2,1,0:T(8,128)(2,1)S(1)} collective-permute-done((bf16[2,104,3584]{2,1,0:T(8,128)(2,1)}, bf16[2,104,3584]{2,1,0:T(8,128)(2,1)S(1)}, u32[]{:S(2)}, u32[]{:S(2)}) %collective-permute-start.4) | collective-permute-done | bytes 1490976 | tf_op jit(solution)/shard_map/ppermute | solution.py:10
  195.5 1.3 fusion.7
  196.8 0.0 all-reduce.3.cloned.1.call-update
  196.8 0.0 reduce-scatter.3.cloned.1.call-start
  196.9 43.3 %all-reduce.3.cloned.1.call-done = (f32[104,256]{1,0:T(8,128)}, f32[104,256]{1,0:T(8,128)}, f32[104,256]{1,0:T(8,128)}) async-done(((f32[104,256]{1,0:T(8,128)}, f32[104,256]{1,0:T(8,128)}, f32[104,256]{1,0:T(8,128)}), (f32[104,256]{1,0:T(8,128)}, f32[104,256]{1,0:T(8,128)}, f32[104,256]{1,0:T(8,128)})) %all-reduce.3.cloned.1.call-update) | async-done | bytes 319504 | tf_op jit(solution)/shard_map/psum | solution.py:47
  240.2 2.9 convolution_convert_fusion.1
  243.1 0.0 reduce-scatter.3.cloned.1.call-update
  243.1 0.0 reduce-scatter.5.cloned.1.call-start
  243.1 0.1 fusion.21
  243.2 3.2 convolution_convert_fusion
  246.4 0.0 reduce-scatter.5.cloned.1.call-update
  246.5 1.8 fusion
  248.2 0.0 collective-permute-start
  248.3 0.9 slice_bitcast_fusion.1
  249.2 1.3 fusion.2
  250.5 10.0 %collective-permute-done = bf16[104,3584]{1,0:T(8,128)(2,1)S(1)} collective-permute-done((bf16[104,3584]{1,0:T(8,128)(2,1)S(1)}, bf16[104,3584]{1,0:T(8,128)(2,1)S(1)}, u32[]{:S(2)}, u32[]{:S(2)}) %collective-permute-start) | collective-permute-done | bytes 745504 | tf_op jit(solution)/shard_map/ppermute | solution.py:16
  260.4 77.6 %reduce-scatter.3.cloned.1.call-done = bf16[16,3584]{1,0:T(8,128)(2,1)} async-done(((bf16[256,3584]{1,0:T(8,128)(2,1)}), bf16[16,3584]{1,0:T(8,128)(2,1)}) %reduce-scatter.3.cloned.1.call-update) | async-done | bytes 114704 | tf_op jit(solution)/shard_map/reduce_scatter | solution.py:63
  338.1 1.6 fusion.13
  339.6 94.1 %reduce-scatter.5.cloned.1.call-done = bf16[16,3584]{1,0:T(8,128)(2,1)} async-done(((bf16[256,3584]{1,0:T(8,128)(2,1)}), bf16[16,3584]{1,0:T(8,128)(2,1)}) %reduce-scatter.5.cloned.1.call-update) | async-done | bytes 114704 | tf_op jit(solution)/shard_map/reduce_scatter | solution.py:66
  433.8 1.6 fusion.14
  435.3 0.9 copy.16
  (19 shorter events, 0.0 us)
Async XLA Ops:
  7.2 2.1 copy-start
  7.2 122.9 %all-gather.7.cloned.1.call-start = ((), (), s32[]{:S(2)}) async-start(), calls=%async_computation.5 | async-start | bytes 1949696 | tf_op jit(solution)/shard_map/all_gather | solution.py:33
  7.9 135.9 %all-gather.5.cloned.1.call-start = ((), (), s32[]{:S(2)}) async-start(), calls=%async_computation.4 | async-start | bytes 1949696 | tf_op jit(solution)/shard_map/all_gather | solution.py:32
  9.3 134.5 %copy-start.11 = (pred[104]{0:T(512)(128)(4,1)}, pred[104]{0:T(512)(128)(4,1)S(1)}, u32[]{:S(2)}) copy-start(pred[104]{0:T(512)(128)(4,1)S(1)} %get-tuple-element.9) | copy-start | bytes 316
  9.3 1.1 copy-start.7
  10.3 1.1 copy-start.8
  10.6 119.5 %copy-start.4 = (bf16[1,1,104,3584]{3,2,1,0:T(8,128)(2,1)S(1)}, bf16[1,1,104,3584]{3,2,1,0:T(8,128)(2,1)}, u32[]{:S(2)}) copy-start(bf16[1,1,104,3584]{3,2,1,0:T(8,128)(2,1)} %param.10) | copy-start | bytes 2236420
  11.6 5.2 %collective-permute-start.1 = (bf16[2,104,3584]{2,1,0:T(8,128)(2,1)S(1)}, bf16[2,104,3584]{2,1,0:T(8,128)(2,1)S(1)}, u32[]{:S(2)}, u32[]{:S(2)}) collective-permute-start(bf16[2,104,3584]{2,1,0:T(8,128)(2,1)S(1)} %pad_maximum_fusion), channel_id=1, source_target_pairs={{0,32},{32,0},{64,96},{96,64},{128,160},{160,128},{192,224},{224,1... | collective-permute-start | bytes 4472840 | tf_op jit(solution)/shard_map/ppermute | solution.py:10
  16.8 36.7 %collective-permute-start.2 = (bf16[2,104,3584]{2,1,0:T(8,128)(2,1)S(1)}, bf16[2,104,3584]{2,1,0:T(8,128)(2,1)}, u32[]{:S(2)}, u32[]{:S(2)}) collective-permute-start(bf16[2,104,3584]{2,1,0:T(8,128)(2,1)S(1)} %collective-permute-done.1), channel_id=1, source_target_pairs={{0,64},{32,96},{64,0},{96,32},{128,192},{160,224},{192,128},{224,1... | collective-permute-start | bytes 4472840 | tf_op jit(solution)/shard_map/ppermute | solution.py:10
  20.3 219.8 %all-reduce.3.cloned.1.call-start = ((), (), s32[]{:S(2)}) async-start(), calls=%async_computation.6 | async-start | bytes 638976 | tf_op jit(solution)/shard_map/psum | solution.py:47
  53.5 68.9 %collective-permute-start.3 = (bf16[2,104,3584]{2,1,0:T(8,128)(2,1)}, bf16[2,104,3584]{2,1,0:T(8,128)(2,1)}, u32[]{:S(2)}, u32[]{:S(2)}) collective-permute-start(bf16[2,104,3584]{2,1,0:T(8,128)(2,1)} %collective-permute-done.2), channel_id=1, source_target_pairs={{0,128},{32,160},{64,192},{96,224},{128,0},{160,32},{192,64},{224,... | collective-permute-start | bytes 4472840 | tf_op jit(solution)/shard_map/ppermute | solution.py:10
  122.4 73.1 %collective-permute-start.4 = (bf16[2,104,3584]{2,1,0:T(8,128)(2,1)}, bf16[2,104,3584]{2,1,0:T(8,128)(2,1)S(1)}, u32[]{:S(2)}, u32[]{:S(2)}) collective-permute-start(bf16[2,104,3584]{2,1,0:T(8,128)(2,1)} %collective-permute-done.3), channel_id=1, source_target_pairs={{0,256},{32,288},{64,320},{96,352},{128,384},{160,416},{192,448},{... | collective-permute-start | bytes 4472840 | tf_op jit(solution)/shard_map/ppermute | solution.py:10
  143.8 51.7 %copy-start.2 = (bf16[1,256,3584]{2,1,0:T(8,128)(2,1)S(1)}, bf16[1,256,3584]{2,1,0:T(8,128)(2,1)}, u32[]{:S(2)}) copy-start(bf16[1,256,3584]{2,1,0:T(8,128)(2,1)} %all-gather.5.cloned.1.call-done) | copy-start | bytes 5505028
  195.5 47.6 %copy-start.5 = (bf16[2,104,3584]{2,1,0:T(8,128)(2,1)}, bf16[2,104,3584]{2,1,0:T(8,128)(2,1)S(1)}, u32[]{:S(2)}) copy-start(bf16[2,104,3584]{2,1,0:T(8,128)(2,1)S(1)} %collective-permute-done.4) | copy-start | bytes 4472836
  196.8 141.3 %reduce-scatter.3.cloned.1.call-start = ((), (), s32[]{:S(2)}) async-start(), calls=%async_computation.2 | async-start | bytes 1949696 | tf_op jit(solution)/shard_map/reduce_scatter | solution.py:63
  240.1 3.0 copy-start.9
  240.1 3.0 copy-start.10
  243.1 190.7 %reduce-scatter.5.cloned.1.call-start = ((), (), s32[]{:S(2)}) async-start(), calls=%async_computation.3 | async-start | bytes 1949696 | tf_op jit(solution)/shard_map/reduce_scatter | solution.py:66
  243.2 3.2 copy-start.1
  246.4 1.8 copy-start.6
  246.4 2.7 copy-start.3
  248.2 12.2 %collective-permute-start = (bf16[104,3584]{1,0:T(8,128)(2,1)S(1)}, bf16[104,3584]{1,0:T(8,128)(2,1)S(1)}, u32[]{:S(2)}, u32[]{:S(2)}) collective-permute-start(bf16[104,3584]{1,0:T(8,128)(2,1)S(1)} %fusion), channel_id=1, source_target_pairs={{0,32},{32,64},{64,96},{96,128},{128,160},{160,192},{192,224},{224... | collective-permute-start | bytes 2236424 | tf_op jit(solution)/shard_map/ppermute | solution.py:16
Sparse Core Ops, SparseCore 0:
  11.1 68.6 all-gather.6
  82.8 60.9 all-gather.4
  197.0 43.1 all-reduce.2
  244.7 93.3 reduce-scatter.2
  342.6 91.1 reduce-scatter.4
where the time goes:
time: 444 us; the launch traced here: 443 us
  waiting for transfers between devices  386 us (87%)
  starting transfers between devices  17.8 us (4%)
  matrix products  16.6 us (4%)
  between operations  14 us (3%)
  other arithmetic  4.87 us (1%)
    ppermute x4, waiting for transfers between devices, partner(): return lax.ppermute(value, axis, pairs)  149 us
    reduce_scatter x1, waiting for transfers between devices, local(): lax.psum_scatter(down_term.astype(jnp.bfloat16), 'dp', scatter_dimension=...  94.1 us
    reduce_scatter x1, waiting for transfers between devices, local(): lax.psum_scatter(up_term.astype(jnp.bfloat16), 'dp', scatter_dimension=0,...  77.6 us
    psum x1, waiting for transfers between devices, local(): lax.psum((fwd_part, bwd_part, slope_part), 'mp')  43.3 us
    ppermute x4, starting transfers between devices, partner(): return lax.ppermute(value, axis, pairs)  17.6 us
    all_gather x1, waiting for transfers between devices, local(): lax.all_gather(w_down[0], 'dp', axis=0, tiled=True)  10.7 us
    ppermute x1, waiting for transfers between devices, passed_along(): return lax.ppermute(value, axis, pairs)  9.95 us
  transfers between devices with their start and end apart: 10, of which 9 were waited for; matrix products, arithmetic and copies ran while one was open for 4% of the time, Pallas kernels for 0%

commit v1 on v0

v1 whole, which is shorter than its diff:
```python
import functools
import math

import jax
import jax.numpy as jnp
from jax import lax
from jax.experimental import pallas as pl
from jax.experimental.pallas import tpu as pltpu
from jax.sharding import PartitionSpec as P

MESH = pl.DeviceIdType.MESH
BF16, F32 = jnp.bfloat16, jnp.float32

D = 3584
R = 256
ROWS = 104
VISION = 24
SHARE = 16
TILE = 256
PIECES = 4
PIECE = D // PIECES
TILES = D // TILE
NX, NZ = 4, 4
SPLIT = 3 * TILE

N_GATHER = 16
N_REDUCE = 12

NT = (((1,), (1,)), ((), ()))
TN = (((0,), (0,)), ((), ()))

SCALE = math.sqrt(2 / math.pi)


def gelu(v):
    return 0.5 * v * (1.0 + jnp.tanh(SCALE * (v + 0.044715 * (v * v * v))))


def gelu_slope(v):
    t = jnp.tanh(SCALE * (v + 0.044715 * (v * v * v)))
    return 0.5 * (1.0 + t) + 0.5 * v * (1.0 - t * t) * (SCALE * (1.0 + 3 * 0.044715 * (v * v)))


def kernel(
    section_ref, vision_ref, alternate_ref, grad_ref, parked_ref, wd_ref, wu_ref,
    o_section, o_parked, o_input_grad, o_up, o_down,
    sec, vis, alt, grad, fwd, bwd, out, weights, parts,
    pre_out, pre_in, act, slope_act, act_t, grad_t,
    opp_up, opp_dn, from_up, from_dn, opp2_up, opp2_dn, from2_up, from2_dn, sums,
    local_sem, g_send, g_recv, r_send, r_recv, m_send, m_recv, y_send, y_recv,
):
    section = lax.axis_index("section")
    dp = lax.axis_index("dp")
    mp = lax.axis_index("mp")
    x, z = lax.div(dp, NZ), lax.rem(dp, NZ)

    def at(value, count):
        return lax.rem(value + count, count)

    def chunk(xi, zi):
        return at(xi, NX) * NZ + at(zi, NZ)

    mirror = {"section": 15 - section}
    following = {"section": lax.rem(section + 1, 16)}
    preceding = {"section": lax.rem(section + 15, 16)}
    other = {"mp": 1 - mp}
    right, left = {"dp": chunk(x + 1, z)}, {"dp": chunk(x - 1, z)}
    plus, minus = {"dp": chunk(x, z + 1)}, {"dp": chunk(x, z - 1)}

    pending = []

    def remote(src, dst, send, recv, to):
        copy = pltpu.make_async_remote_copy(
            src_ref=src, dst_ref=dst, send_sem=send, recv_sem=recv,
            device_id=to, device_id_type=MESH,
        )
        return copy

    def go(copy):
        copy.start()
        pending.append(copy)

    w_refs = (wd_ref, wu_ref)
    loads = [
        pltpu.make_async_copy(section_ref, sec, local_sem.at[0]),
        pltpu.make_async_copy(vision_ref, vis, local_sem.at[1]),
        pltpu.make_async_copy(alternate_ref, alt, local_sem.at[2]),
        pltpu.make_async_copy(grad_ref, grad, local_sem.at[3]),
        pltpu.make_async_copy(wd_ref, weights.at[0, x, z], local_sem.at[4]),
        pltpu.make_async_copy(wu_ref, weights.at[1, x, z], local_sem.at[5]),
    ]
    for load in loads:
        load.start()

    barrier = pltpu.get_barrier_semaphore()
    for partner in (mirror, following, preceding, other, right, left, plus, minus):
        pl.semaphore_signal(barrier, inc=1, device_id=partner, device_id_type=MESH)
    pl.semaphore_wait(barrier, 8)

    def y_piece(src, dst, index, piece, to):
        cols = pl.ds(piece * PIECE, PIECE)
        return remote(
            src.at[:, cols], dst.at[:, cols], y_send.at[index], y_recv.at[index], to
        )

    parked_copies = [y_piece(parked_ref, bwd, i, i, mirror) for i in range(PIECES)]
    forward_copies = [y_piece(fwd, o_parked, PIECES + i, i, mirror) for i in range(PIECES)]
    shift_copies = [y_piece(out, o_section, 2 * PIECES + i, i, following) for i in range(PIECES)]
    for copy in parked_copies:
        go(copy)

    def forward_behind_parked(i):
        parked_copies[i].wait_recv()
        go(forward_copies[i])

    class Gather:
        def __init__(self, number, w, start, stop, x_first):
            self.base, self.w, self.start, self.stop = number * N_GATHER, w, start, stop
            self.x_first = x_first
            self.a, self.b = (x, z) if x_first else (z, x)
            xs, zs = (right, left), (plus, minus)
            (self.up, self.dn), (self.up2, self.dn2) = (xs, zs) if x_first else (zs, xs)
            middle = (start + stop) // 2
            self.all = pl.ds(start, stop - start)
            self.low, self.high = pl.ds(start, middle - start), pl.ds(middle, stop - middle)

        def copy(self, m, to, a=0, b=0, cols=None):
            cols = self.all if cols is None else cols
            a, b = at(self.a + a, 4), at(self.b + b, 4)
            xi, zi = (a, b) if self.x_first else (b, a)
            place = weights.at[self.w, xi, zi, :, cols]
            index = self.base + m
            return remote(place, place, g_send.at[index], g_recv.at[index], to)

        def start1(self):
            go(self.copy(0, self.up))
            go(self.copy(1, self.dn))

        def start2(self, k):
            go(self.copy(4 + k, self.up2, a=k))
            go(self.copy(8 + k, self.dn2, a=k))

        def near1(self):
            self.copy(0, self.up).wait_recv()
            go(self.copy(2, self.up, a=-1, cols=self.low))
            self.start2(3)
            self.copy(1, self.dn).wait_recv()
            go(self.copy(3, self.dn, a=1, cols=self.high))
            self.start2(1)

        def far1(self):
            self.copy(2, self.up, cols=self.low).wait_recv()
            self.copy(3, self.dn, cols=self.high).wait_recv()
            self.start2(2)

        def near2(self, k):
            self.copy(4 + k, self.up2).wait_recv()
            if k % 2 == 0:
                go(self.copy(12 + k // 2, self.up2, a=k, b=-1))
            self.copy(8 + k, self.dn2).wait_recv()
            if k % 2 == 1:
                go(self.copy(14 + k // 2, self.dn2, a=k, b=1))

        def far2(self, k):
            if k % 2 == 0:
                self.copy(12 + k // 2, self.up2).wait_recv()
            else:
                self.copy(14 + k // 2, self.dn2).wait_recv()

    down = Gather(0, 0, SPLIT, D, False)
    up = Gather(1, 1, SPLIT, D, False)
    both = Gather(2, slice(None), 0, SPLIT, True)

    def tile(i):
        return pl.ds(pl.multiple_of(i * TILE, TILE), TILE)

    def exchange(slot):
        return remote(
            pre_out.at[slot], pre_in.at[slot], m_send.at[slot], m_recv.at[slot], other
        )

    def weight(w, cols):
        block = weights[w, :, :, :, cols]
        return block.reshape(R, block.shape[-1])

    def partial(slot, rows, w):
        def body(i, total):
            cols = pl.ds(pl.multiple_of(i * 512, 512), 512)
            return total + lax.dot_general(
                rows[:, cols], weight(w, cols), NT, preferred_element_type=F32
            )

        total = lax.fori_loop(0, D // 512, body, jnp.zeros((ROWS, R), F32))
        pre_out[slot] = total.astype(BF16)
        go(exchange(slot))

    def summed(slot):
        exchange(slot).wait_recv()
        return pre_out[slot].astype(F32) + pre_in[slot].astype(F32)

    for load in loads[4:]:
        load.wait()
    down.start1()
    down.start2(0)
    both.start1()
    both.start2(0)
    up.start2(0)

    for load in loads[:3]:
        load.wait()
    picks = jnp.where(section == 0, alt[...], -1)
    chosen_t = (lax.broadcasted_iota(jnp.int32, (VISION, ROWS), 0) == picks).astype(BF16)
    hit = lax.dot_general(
        chosen_t, jnp.ones((VISION, TILE), BF16), TN, preferred_element_type=F32
    )

    def choose(i, carry):
        cols = tile(i)
        chosen = lax.dot_general(chosen_t, vis[:, cols], TN, preferred_element_type=F32)
        fwd[:, cols] = jnp.where(hit > 0.5, chosen, sec[:, cols].astype(F32)).astype(BF16)
        return carry

    lax.fori_loop(0, TILES, choose, 0)

    down.near1()
    up.start1()
    both.near1()
    down.near2(0)
    both.far1()
    both.near2(0)
    down.far1()
    down.near2(3)
    down.near2(1)
    both.near2(3)
    both.near2(1)
    up.near1()
    down.far2(0)
    down.near2(2)
    up.far1()
    both.near2(2)
    up.near2(0)
    up.near2(3)
    up.near2(1)
    up.far2(0)
    up.near2(2)
    forward_behind_parked(0)
    forward_behind_parked(1)
    for k in (3, 1, 2):
        down.far2(k)
    for k in (0, 3, 1, 2):
        both.far2(k)
    partial(0, fwd, 0)
    forward_behind_parked(2)
    forward_behind_parked(3)
    partial(2, bwd, 0)
    for k in (3, 1, 2):
        up.far2(k)
    loads[3].wait()
    partial(1, grad, 1)

    bwd_pre = summed(2)
    bwd_act = gelu(bwd_pre).astype(BF16)
    act_t[...] = bwd_act.T
    pre_grad = (summed(1) * gelu_slope(bwd_pre)).astype(BF16)
    slope_act[...] = pre_grad
    grad_t[...] = pre_grad.T

    def output(i, carry):
        cols = pl.ds(pl.multiple_of(i * 128, 128), 128)
        product = jnp.dot(act[...], weight(1, cols), preferred_element_type=F32)
        out[:, cols] = (fwd[:, cols].astype(F32) + product).astype(BF16)
        return carry

    def outputs():
        act[...] = gelu(summed(0)).astype(BF16)
        for i in range(PIECES):
            lax.fori_loop(i * PIECE // 128, (i + 1) * PIECE // 128, output, 0)
            go(shift_copies[i])

    def add_into(total, term):
        total[...] = (total[...].astype(F32) + term[...].astype(F32)).astype(BF16)

    class Reduce:
        def __init__(self, number, w, start, stop, x_first):
            self.base, self.w, self.start, self.stop = number * N_REDUCE, w, start, stop
            self.x_first = x_first
            self.a, self.b = (x, z) if x_first else (z, x)
            xs, zs = (right, left), (plus, minus)
            (self.up, self.dn), (self.up2, self.dn2) = (xs, zs) if x_first else (zs, xs)
            middle = (start + stop) // 2
            self.all = pl.ds(start, stop - start)
            self.low, self.high = pl.ds(start, middle - start), pl.ds(middle, stop - middle)

        def block(self, a, b0, count):
            a = at(self.a + a, 4)
            if self.x_first:
                return parts.at[self.w, a, pl.ds(b0, count), :, self.all]
            return parts.at[self.w, pl.ds(b0, count), a, :, self.all]

        def term(self, ref, b0, count):
            return ref.at[self.w, pl.ds(b0, count), :, self.all]

        def total(self, b, cols):
            return sums.at[self.w, at(self.b + b, 4), :, cols]

        def copy(self, m):
            w = self.w
            src, dst, to = (
                lambda: (self.block(2, 0, 2), self.term(opp_up, 0, 2), self.dn),
                lambda: (self.block(2, 2, 2), self.term(opp_dn, 0, 2), self.up),
                lambda: (self.block(-1, 2, 2), self.term(from_up, 2, 2), self.dn),
                lambda: (self.block(1, 0, 2), self.term(from_dn, 0, 2), self.up),
                lambda: (self.block(-1, 0, 2), self.term(from_up, 0, 2), self.dn),
                lambda: (self.block(1, 2, 2), self.term(from_dn, 2, 2), self.up),
                lambda: (self.total(2, self.low), opp2_up.at[w, :, self.low], self.dn2),
                lambda: (self.total(2, self.high), opp2_dn.at[w, :, self.high], self.up2),
                lambda: (self.total(-1, self.high), from2_up.at[w, :, self.high], self.dn2),
                lambda: (self.total(1, self.low), from2_dn.at[w, :, self.low], self.up2),
                lambda: (self.total(-1, self.low), from2_up.at[w, :, self.low], self.dn2),
                lambda: (self.total(1, self.high), from2_dn.at[w, :, self.high], self.up2),
            )[m]()
            index = self.base + m
            return remote(src, dst, r_send.at[index], r_recv.at[index], to)

        def stage_a(self):
            lhs, rhs = ((act_t, grad), (grad_t, bwd))[self.w]

            def body(i, carry):
                cols = tile(i)
                product = jnp.dot(lhs[...], rhs[:, cols], preferred_element_type=F32)
                parts[self.w, :, :, :, cols] = product.astype(BF16).reshape(NX, NZ, SHARE, TILE)
                return carry

            lax.fori_loop(self.start // TILE, self.stop // TILE, body, 0)
            for m in range(4):
                go(self.copy(m))

        def stage_b(self):
            self.copy(0).wait_recv()
            add_into(self.block(-1, 0, 2), self.term(opp_up, 0, 2))
            go(self.copy(4))
            self.copy(1).wait_recv()
            add_into(self.block(1, 2, 2), self.term(opp_dn, 0, 2))
            go(self.copy(5))

        def stage_c(self):
            for m in (2, 3, 4, 5):
                self.copy(m).wait_recv()
            self.term(sums, 0, 4)[...] = (
                self.block(0, 0, 4)[...].astype(F32)
                + self.term(from_up, 0, 4)[...].astype(F32)
                + self.term(from_dn, 0, 4)[...].astype(F32)
            ).astype(BF16)
            for m in (6, 7, 8, 9):
                go(self.copy(m))

        def stage_d(self):
            w = self.w
            self.copy(6).wait_recv()
            add_into(self.total(-1, self.low), opp2_up.at[w, :, self.low])
            go(self.copy(10))
            self.copy(7).wait_recv()
            add_into(self.total(1, self.high), opp2_dn.at[w, :, self.high])
            go(self.copy(11))

        def stage_e(self):
            w, cols = self.w, self.all
            for m in (8, 9, 10, 11):
                self.copy(m).wait_recv()
            total = (
                parts[w, x, z, :, cols].astype(F32)
                + from_up[w, self.b, :, cols].astype(F32)
                + from_dn[w, self.b, :, cols].astype(F32)
                + from2_up[w, :, cols].astype(F32)
                + from2_dn[w, :, cols].astype(F32)
            )
            (o_up, o_down)[w][:, cols] = (total * (1.0 / 16)).astype(BF16)

    def input_grad(i, carry):
        cols = tile(i)
        product = jnp.dot(slope_act[...], weight(0, cols), preferred_element_type=F32)
        o_input_grad[:, cols] = (grad[:, cols].astype(F32) + product).astype(BF16)
        return carry

    cut = SPLIT + 6 * TILE
    u0, u1 = Reduce(0, 0, SPLIT, cut, True), Reduce(1, 0, cut, D, True)
    d0, d1 = Reduce(2, 1, SPLIT, cut, True), Reduce(3, 1, cut, D, True)
    uz, dz = Reduce(4, 0, 0, SPLIT, False), Reduce(5, 1, 0, SPLIT, False)
    u0.stage_a()
    uz.stage_a()
    u1.stage_a()
    u0.stage_b()
    uz.stage_b()
    outputs()
    d0.stage_a()
    dz.stage_a()
    u1.stage_b()
    u0.stage_c()
    uz.stage_c()
    d1.stage_a()
    lax.fori_loop(0, TILES, input_grad, 0)
    d0.stage_b()
    u0.stage_d()
    uz.stage_d()
    dz.stage_b()
    u1.stage_c()
    u1.stage_d()
    dz.stage_c()
    u0.stage_e()
    uz.stage_e()
    d1.stage_b()
    d0.stage_c()
    dz.stage_d()
    d0.stage_d()
    u1.stage_e()
    d1.stage_c()
    d1.stage_d()
    dz.stage_e()
    d0.stage_e()
    d1.stage_e()

    for copy in forward_copies + shift_copies:
        copy.wait_recv()
    for copy in pending:
        copy.wait_send()


def write_out(*refs):
    copies = [
        pltpu.make_async_copy(refs[i], refs[5 + i], refs[10].at[i]) for i in range(5)
    ]
    for copy in copies:
        copy.start()
    for copy in copies:
        copy.wait()


def local(section_in, vision_rows, alternate, grad_in, parked, w_down, w_up):
    rows = jax.ShapeDtypeStruct((ROWS, D), BF16)
    shares = jax.ShapeDtypeStruct((SHARE, D), BF16)
    dma = pltpu.SemaphoreType.DMA
    outs = pl.pallas_call(
        kernel,
        out_shape=(pltpu.VMEM((ROWS, D), BF16),) * 3 + (pltpu.VMEM((SHARE, D), BF16),) * 2,
        in_specs=[pl.BlockSpec(memory_space=pltpu.HBM)] * 7,
        out_specs=[pl.BlockSpec(memory_space=pltpu.VMEM)] * 5,
        scratch_shapes=[
            pltpu.VMEM((ROWS, D), BF16),
            pltpu.VMEM((VISION, D), BF16),
            pltpu.VMEM((1, ROWS), jnp.int32),
            pltpu.VMEM((ROWS, D), BF16),
            pltpu.VMEM((ROWS, D), BF16),
            pltpu.VMEM((ROWS, D), BF16),
            pltpu.VMEM((ROWS, D), BF16),
            pltpu.VMEM((2, NX, NZ, SHARE, D), BF16),
            pltpu.VMEM((2, NX, NZ, SHARE, D), BF16),
            pltpu.VMEM((3, ROWS, R), BF16),
            pltpu.VMEM((3, ROWS, R), BF16),
            pltpu.VMEM((ROWS, R), BF16),
            pltpu.VMEM((ROWS, R), BF16),
            pltpu.VMEM((R, ROWS), BF16),
            pltpu.VMEM((R, ROWS), BF16),
            pltpu.VMEM((2, 2, SHARE, D), BF16),
            pltpu.VMEM((2, 2, SHARE, D), BF16),
            pltpu.VMEM((2, 4, SHARE, D), BF16),
            pltpu.VMEM((2, 4, SHARE, D), BF16),
            pltpu.VMEM((2, SHARE, D), BF16),
            pltpu.VMEM((2, SHARE, D), BF16),
            pltpu.VMEM((2, SHARE, D), BF16),
            pltpu.VMEM((2, SHARE, D), BF16),
            pltpu.VMEM((2, 4, SHARE, D), BF16),
            dma((6,)),
            dma((3 * N_GATHER,)),
            dma((3 * N_GATHER,)),
            dma((6 * N_REDUCE,)),
            dma((6 * N_REDUCE,)),
            dma((3,)),
            dma((3,)),
            dma((3 * PIECES,)),
            dma((3 * PIECES,)),
        ],
        compiler_params=pltpu.CompilerParams(
            collective_id=0, has_side_effects=True, vmem_limit_bytes=40 * 2**20
        ),
        cost_estimate=pl.CostEstimate(
            flops=14 * ROWS * D * R, bytes_accessed=12 * ROWS * D, transcendentals=3 * ROWS * R
        ),
        name="relay_tick",
    )(*(
        pltpu.with_memory_space_constraint(operand, pltpu.HBM)
        for operand in (
            section_in[0, 0], vision_rows[0], alternate, grad_in[0, 0], parked[0, 0],
            w_down[0], w_up[0],
        )
    ))
    received, stash, input_grad, up_grad, down_grad = pl.pallas_call(
        write_out,
        out_shape=(rows, rows, rows, shares, shares),
        in_specs=[pl.BlockSpec(memory_space=pltpu.VMEM)] * 5,
        out_specs=[pl.BlockSpec(memory_space=pltpu.HBM)] * 5,
        scratch_shapes=[dma((5,))],
        name="write_out",
    )(*(pltpu.with_memory_space_constraint(out, pltpu.VMEM) for out in outs))
    return (
        received[None, None],
        stash[None, None],
        input_grad[None, None],
        up_grad[None],
        down_grad[None],
    )


def solution(mesh):
    rows = P("section", "dp", None, "mp")
    shares = P("section", "dp", "mp")
    return jax.shard_map(
        local,
        mesh=mesh,
        in_specs=(rows, P("dp", None, "mp"), P("dp", None), rows, rows, shares, shares),
        out_specs=(rows, rows, rows, shares, shares),
        check_vma=False,
    )
```

time: 444 us -> 115 us (0.26)
  the two profiles are of different devices: /device:TPU:6 before, /device:TPU:24 now
where the time goes in v1:
time: 115 us; the launch traced here: 114 us
  Pallas kernels  114 us (99%)
    pallas_call x1, Pallas kernels, local(): pl.pallas_call(kernel, out_shape=(pltpu.VMEM((ROWS, D), BF16),) * 3 + (pl...  112 us

profile of v1, /device:TPU:24, one launch (start us, length us, event | category | flops | bytes accessed | tf_op | source)
XLA Modules:
  0.0 114.4 jit_solution(11358953147903188770)
XLA Ops:
  0.6 112.3 %relay_tick.1 = (bf16[104,3584]{1,0:T(8,128)(2,1)S(1)}, bf16[104,3584]{1,0:T(8,128)(2,1)S(1)}, bf16[104,3584]{1,0:T(8,128)(2,1)S(1)}, bf16[16,3584]{1,0:T(8,128)(2,1)S(1)}, bf16[16,3584]{1,0:T(8,128)(2,1)S(1)}) custom-call(bf16[104,3584]{1,0:T(8,128)(2,1)} %bitcast.11, bf16[24,3584]{1,0:T(8,128)(2,1)} %bitcast.17, s32[1,104]{1,0:T(1,128)} %alternate_ref.1, ...), custom_call_target="tpu_custom_call" | custom-call | flops 1335885824 | bytes 4472832 | tf_op jit(solution)/shard_map/relay_tick/pallas_call | solution.py:442
  113.0 1.5 %write_out.1 = (bf16[104,3584]{1,0:T(8,128)(2,1)}, bf16[104,3584]{1,0:T(8,128)(2,1)}, bf16[104,3584]{1,0:T(8,128)(2,1)}, bf16[16,3584]{1,0:T(8,128)(2,1)}, bf16[16,3584]{1,0:T(8,128)(2,1)}) custom-call(bf16[104,3584]{1,0:T(8,128)(2,1)S(1)} %get-tuple-element.15.refs_0_, bf16[104,3584]{1,0:T(8,128)(2,1)S(1)} %get-tuple-element.16.refs_1_, ...), custom_call_target="tpu_custom_call" | custom-call | tf_op jit(solution)/shard_map/write_out/pallas_call | solution.py:496

commit v2 on v1

--- a/solution.py
+++ b/solution.py
@@ -109,9 +109,14 @@
     for copy in parked_copies:
         go(copy)
 
-    def forward_behind_parked(i):
-        parked_copies[i].wait_recv()
-        go(forward_copies[i])
+    y = lax.div(section, 2)
+    near = jnp.logical_or(lax.rem(y, 4) == 0, lax.rem(y, 4) == 3)
+
+    def send_forward(pieces, when):
+        @pl.when(when)
+        def _():
+            for i in pieces:
+                forward_copies[i].start()
 
     class Gather:
         def __init__(self, number, w, start, stop, x_first):
@@ -190,7 +195,9 @@
                 rows[:, cols], weight(w, cols), NT, preferred_element_type=F32
             )
 
-        total = lax.fori_loop(0, D // 512, body, jnp.zeros((ROWS, R), F32))
+        send_partial(slot, lax.fori_loop(0, D // 512, body, jnp.zeros((ROWS, R), F32)))
+
+    def send_partial(slot, total):
         pre_out[slot] = total.astype(BF16)
         go(exchange(slot))
 
@@ -243,20 +250,23 @@
     up.near2(1)
     up.far2(0)
     up.near2(2)
-    forward_behind_parked(0)
-    forward_behind_parked(1)
     for k in (3, 1, 2):
         down.far2(k)
     for k in (0, 3, 1, 2):
         both.far2(k)
     partial(0, fwd, 0)
-    forward_behind_parked(2)
-    forward_behind_parked(3)
-    partial(2, bwd, 0)
     for k in (3, 1, 2):
         up.far2(k)
     loads[3].wait()
     partial(1, grad, 1)
+
+    total = jnp.zeros((ROWS, R), F32)
+    for i in range(PIECES):
+        parked_copies[i].wait_recv()
+        send_forward([i], near)
+        cols = pl.ds(i * PIECE, PIECE)
+        total += lax.dot_general(bwd[:, cols], weight(0, cols), NT, preferred_element_type=F32)
+    send_partial(2, total)
 
     bwd_pre = summed(2)
     bwd_act = gelu(bwd_pre).astype(BF16)
@@ -271,11 +281,9 @@
         out[:, cols] = (fwd[:, cols].astype(F32) + product).astype(BF16)
         return carry
 
-    def outputs():
-        act[...] = gelu(summed(0)).astype(BF16)
-        for i in range(PIECES):
-            lax.fori_loop(i * PIECE // 128, (i + 1) * PIECE // 128, output, 0)
-            go(shift_copies[i])
+    def outputs(i):
+        lax.fori_loop(i * PIECE // 128, (i + 1) * PIECE // 128, output, 0)
+        go(shift_copies[i])
 
     def add_into(total, term):
         total[...] = (total[...].astype(F32) + term[...].astype(F32)).astype(BF16)
@@ -389,30 +397,36 @@
     u0.stage_a()
     uz.stage_a()
     u1.stage_a()
+    act[...] = gelu(summed(0)).astype(BF16)
     u0.stage_b()
+    send_forward(range(PIECES), jnp.logical_not(near))
     uz.stage_b()
-    outputs()
     d0.stage_a()
+    outputs(0)
     dz.stage_a()
     u1.stage_b()
     u0.stage_c()
     uz.stage_c()
+    outputs(1)
     d1.stage_a()
-    lax.fori_loop(0, TILES, input_grad, 0)
+    outputs(2)
     d0.stage_b()
     u0.stage_d()
     uz.stage_d()
+    outputs(3)
     dz.stage_b()
     u1.stage_c()
     u1.stage_d()
     dz.stage_c()
+    lax.fori_loop(0, TILES // 2, input_grad, 0)
+    d1.stage_b()
+    d0.stage_c()
     u0.stage_e()
     uz.stage_e()
-    d1.stage_b()
-    d0.stage_c()
     dz.stage_d()
     d0.stage_d()
     u1.stage_e()
+    lax.fori_loop(TILES // 2, TILES, input_grad, 0)
     d1.stage_c()
     d1.stage_d()
     dz.stage_e()
@@ -421,7 +435,7 @@
 
     for copy in forward_copies + shift_copies:
         copy.wait_recv()
-    for copy in pending:
+    for copy in pending + forward_copies:
         copy.wait_send()
 
 

time: 115 us -> 102 us (0.89)
  the two profiles are of different devices: /device:TPU:24 before, /device:TPU:6 now
where the time goes in v2:
time: 102 us; the launch traced here: 100 us
  Pallas kernels  99.6 us (98%)
    pallas_call x1, Pallas kernels, local(): pl.pallas_call(kernel, out_shape=(pltpu.VMEM((ROWS, D), BF16),) * 3 + (pl...  98.1 us

profile of v2, /device:TPU:6, one launch (start us, length us, event | category | flops | bytes accessed | tf_op | source)
XLA Modules:
  0.0 100.2 jit_solution(4295576512039121686)
XLA Ops:
  0.6 98.1 %relay_tick.1 = (bf16[104,3584]{1,0:T(8,128)(2,1)S(1)}, bf16[104,3584]{1,0:T(8,128)(2,1)S(1)}, bf16[104,3584]{1,0:T(8,128)(2,1)S(1)}, bf16[16,3584]{1,0:T(8,128)(2,1)S(1)}, bf16[16,3584]{1,0:T(8,128)(2,1)S(1)}) custom-call(bf16[104,3584]{1,0:T(8,128)(2,1)} %bitcast.11, bf16[24,3584]{1,0:T(8,128)(2,1)} %bitcast.17, s32[1,104]{1,0:T(1,128)} %alternate_ref.1, ...), custom_call_target="tpu_custom_call" | custom-call | flops 1335885824 | bytes 4472832 | tf_op jit(solution)/shard_map/relay_tick/pallas_call | solution.py:456
  98.8 1.5 %write_out.1 = (bf16[104,3584]{1,0:T(8,128)(2,1)}, bf16[104,3584]{1,0:T(8,128)(2,1)}, bf16[104,3584]{1,0:T(8,128)(2,1)}, bf16[16,3584]{1,0:T(8,128)(2,1)}, bf16[16,3584]{1,0:T(8,128)(2,1)}) custom-call(bf16[104,3584]{1,0:T(8,128)(2,1)S(1)} %get-tuple-element.15.refs_0_, bf16[104,3584]{1,0:T(8,128)(2,1)S(1)} %get-tuple-element.16.refs_1_, ...), custom_call_target="tpu_custom_call" | custom-call | tf_op jit(solution)/shard_map/write_out/pallas_call | solution.py:510

commit v3 on v2

--- a/solution.py
+++ b/solution.py
@@ -19,7 +19,6 @@
 TILE = 256
 PIECES = 4
 PIECE = D // PIECES
-TILES = D // TILE
 NX, NZ = 4, 4
 SPLIT = 3 * TILE
 
@@ -176,8 +175,8 @@
     up = Gather(1, 1, SPLIT, D, False)
     both = Gather(2, slice(None), 0, SPLIT, True)
 
-    def tile(i):
-        return pl.ds(pl.multiple_of(i * TILE, TILE), TILE)
+    def piece(i):
+        return pl.ds(i * PIECE, PIECE)
 
     def exchange(slot):
         return remote(
@@ -189,13 +188,12 @@
         return block.reshape(R, block.shape[-1])
 
     def partial(slot, rows, w):
-        def body(i, total):
-            cols = pl.ds(pl.multiple_of(i * 512, 512), 512)
-            return total + lax.dot_general(
-                rows[:, cols], weight(w, cols), NT, preferred_element_type=F32
+        total = jnp.zeros((ROWS, R), F32)
+        for i in range(PIECES):
+            total += lax.dot_general(
+                rows[:, piece(i)], weight(w, piece(i)), NT, preferred_element_type=F32
             )
-
-        send_partial(slot, lax.fori_loop(0, D // 512, body, jnp.zeros((ROWS, R), F32)))
+        send_partial(slot, total)
 
     def send_partial(slot, total):
         pre_out[slot] = total.astype(BF16)
@@ -218,16 +216,13 @@
     picks = jnp.where(section == 0, alt[...], -1)
     chosen_t = (lax.broadcasted_iota(jnp.int32, (VISION, ROWS), 0) == picks).astype(BF16)
     hit = lax.dot_general(
-        chosen_t, jnp.ones((VISION, TILE), BF16), TN, preferred_element_type=F32
+        chosen_t, jnp.ones((VISION, PIECE), BF16), TN, preferred_element_type=F32
     )
 
-    def choose(i, carry):
-        cols = tile(i)
+    for i in range(PIECES):
+        cols = piece(i)
         chosen = lax.dot_general(chosen_t, vis[:, cols], TN, preferred_element_type=F32)
         fwd[:, cols] = jnp.where(hit > 0.5, chosen, sec[:, cols].astype(F32)).astype(BF16)
-        return carry
-
-    lax.fori_loop(0, TILES, choose, 0)
 
     down.near1()
     up.start1()
@@ -264,7 +259,7 @@
     for i in range(PIECES):
         parked_copies[i].wait_recv()
         send_forward([i], near)
-        cols = pl.ds(i * PIECE, PIECE)
+        cols = piece(i)
         total += lax.dot_general(bwd[:, cols], weight(0, cols), NT, preferred_element_type=F32)
     send_partial(2, total)
 
@@ -275,14 +270,10 @@
     slope_act[...] = pre_grad
     grad_t[...] = pre_grad.T
 
-    def output(i, carry):
-        cols = pl.ds(pl.multiple_of(i * 128, 128), 128)
+    def outputs(i):
+        cols = piece(i)
         product = jnp.dot(act[...], weight(1, cols), preferred_element_type=F32)
         out[:, cols] = (fwd[:, cols].astype(F32) + product).astype(BF16)
-        return carry
-
-    def outputs(i):
-        lax.fori_loop(i * PIECE // 128, (i + 1) * PIECE // 128, output, 0)
         go(shift_copies[i])
 
     def add_into(total, term):
@@ -333,13 +324,12 @@
         def stage_a(self):
             lhs, rhs = ((act_t, grad), (grad_t, bwd))[self.w]
 
-            def body(i, carry):
-                cols = tile(i)
+            steps = max(1, (self.stop - self.start) // 640)
+            width = (self.stop - self.start) // steps
+            for i in range(steps):
+                cols = pl.ds(self.start + i * width, width)
                 product = jnp.dot(lhs[...], rhs[:, cols], preferred_element_type=F32)
-                parts[self.w, :, :, :, cols] = product.astype(BF16).reshape(NX, NZ, SHARE, TILE)
-                return carry
-
-            lax.fori_loop(self.start // TILE, self.stop // TILE, body, 0)
+                parts[self.w, :, :, :, cols] = product.astype(BF16).reshape(NX, NZ, SHARE, width)
             for m in range(4):
                 go(self.copy(m))
 
@@ -384,11 +374,10 @@
             )
             (o_up, o_down)[w][:, cols] = (total * (1.0 / 16)).astype(BF16)
 
-    def input_grad(i, carry):
-        cols = tile(i)
+    def input_grad(i):
+        cols = piece(i)
         product = jnp.dot(slope_act[...], weight(0, cols), preferred_element_type=F32)
         o_input_grad[:, cols] = (grad[:, cols].astype(F32) + product).astype(BF16)
-        return carry
 
     cut = SPLIT + 6 * TILE
     u0, u1 = Reduce(0, 0, SPLIT, cut, True), Reduce(1, 0, cut, D, True)
@@ -418,7 +407,8 @@
     u1.stage_c()
     u1.stage_d()
     dz.stage_c()
-    lax.fori_loop(0, TILES // 2, input_grad, 0)
+    input_grad(0)
+    input_grad(1)
     d1.stage_b()
     d0.stage_c()
     u0.stage_e()
@@ -426,7 +416,8 @@
     dz.stage_d()
     d0.stage_d()
     u1.stage_e()
-    lax.fori_loop(TILES // 2, TILES, input_grad, 0)
+    input_grad(2)
+    input_grad(3)
     d1.stage_c()
     d1.stage_d()
     dz.stage_e()

time: 102 us -> 98.7 us (0.968); the launches traced: 100 us -> 98.5 us
  Pallas kernels: 99.6 us -> 97.8 us
    pallas_call x1, Pallas kernels: 98.1 us -> 96.4 us  [local(): pl.pallas_call(kernel, out_shape=(pltpu.VMEM((ROWS, D), BF16),) * 3 + (pl...]
where the time goes in v3:
time: 98.7 us; the launch traced here: 98.5 us
  Pallas kernels  97.8 us (99%)
    pallas_call x1, Pallas kernels, local(): pl.pallas_call(kernel, out_shape=(pltpu.VMEM((ROWS, D), BF16),) * 3 + (pl...  96.4 us

profile of v3, /device:TPU:6, one launch (start us, length us, event | category | flops | bytes accessed | tf_op | source)
XLA Modules:
  0.0 98.5 jit_solution(14615306130188820854)
XLA Ops:
  0.6 96.4 %relay_tick.1 = (bf16[104,3584]{1,0:T(8,128)(2,1)S(1)}, bf16[104,3584]{1,0:T(8,128)(2,1)S(1)}, bf16[104,3584]{1,0:T(8,128)(2,1)S(1)}, bf16[16,3584]{1,0:T(8,128)(2,1)S(1)}, bf16[16,3584]{1,0:T(8,128)(2,1)S(1)}) custom-call(bf16[104,3584]{1,0:T(8,128)(2,1)} %bitcast.11, bf16[24,3584]{1,0:T(8,128)(2,1)} %bitcast.17, s32[1,104]{1,0:T(1,128)} %alternate_ref.1, ...), custom_call_target="tpu_custom_call" | custom-call | flops 1335885824 | bytes 4472832 | tf_op jit(solution)/shard_map/relay_tick/pallas_call | solution.py:447
  97.0 1.5 %write_out.1 = (bf16[104,3584]{1,0:T(8,128)(2,1)}, bf16[104,3584]{1,0:T(8,128)(2,1)}, bf16[104,3584]{1,0:T(8,128)(2,1)}, bf16[16,3584]{1,0:T(8,128)(2,1)}, bf16[16,3584]{1,0:T(8,128)(2,1)}) custom-call(bf16[104,3584]{1,0:T(8,128)(2,1)S(1)} %get-tuple-element.15.refs_0_, bf16[104,3584]{1,0:T(8,128)(2,1)S(1)} %get-tuple-element.16.refs_1_, ...), custom_call_target="tpu_custom_call" | custom-call | tf_op jit(solution)/shard_map/write_out/pallas_call | solution.py:501

commit v4 on v3

--- a/solution.py
+++ b/solution.py
@@ -45,7 +45,7 @@
     o_section, o_parked, o_input_grad, o_up, o_down,
     sec, vis, alt, grad, fwd, bwd, out, weights, parts,
     pre_out, pre_in, act, slope_act, act_t, grad_t,
-    opp_up, opp_dn, from_up, from_dn, opp2_up, opp2_dn, from2_up, from2_dn, sums,
+    stop, opp_up, opp_dn, from_up, from_dn, opp2_up, opp2_dn, from2_up, from2_dn, sums,
     local_sem, g_send, g_recv, r_send, r_recv, m_send, m_recv, y_send, y_recv,
 ):
     section = lax.axis_index("section")
@@ -91,15 +91,35 @@
     for load in loads:
         load.start()
 
+    y, core = lax.div(section, 2), lax.rem(section, 2)
+    turn = lax.rem(y, 4)
+    near = jnp.logical_or(turn == 0, turn == 3)
+    far = jnp.logical_not(near)
+    detours, stops, ends = turn == 2, turn == 0, turn == 1
+    stop_at = {"section": lax.rem(section + 12, 16)}
+    stop_from = {"section": lax.rem(section + 4, 16)}
+    stop_to = {"section": lax.rem(y + 5, 8) * 2 + 1 - core}
+    end_from = {"section": lax.rem(y + 3, 8) * 2 + 1 - core}
+
     barrier = pltpu.get_barrier_semaphore()
-    for partner in (mirror, following, preceding, other, right, left, plus, minus):
-        pl.semaphore_signal(barrier, inc=1, device_id=partner, device_id_type=MESH)
-    pl.semaphore_wait(barrier, 8)
-
-    def y_piece(src, dst, index, piece, to):
-        cols = pl.ds(piece * PIECE, PIECE)
+
+    def greet(*partners):
+        for partner in partners:
+            pl.semaphore_signal(barrier, inc=1, device_id=partner, device_id_type=MESH)
+
+    greet(mirror, following, preceding, other, right, left, plus, minus)
+    pl.when(detours)(lambda: greet(stop_at))
+    pl.when(stops)(lambda: greet(stop_from, stop_to))
+    pl.when(ends)(lambda: greet(end_from))
+    extra = jnp.where(stops, 2, jnp.where(turn == 3, 0, 1))
+    pl.semaphore_wait(barrier, 8 + extra)
+
+    def piece(i):
+        return pl.ds(i * PIECE, PIECE)
+
+    def y_piece(src, dst, index, i, to):
         return remote(
-            src.at[:, cols], dst.at[:, cols], y_send.at[index], y_recv.at[index], to
+            src.at[:, piece(i)], dst.at[:, piece(i)], y_send.at[index], y_recv.at[index], to
         )
 
     parked_copies = [y_piece(parked_ref, bwd, i, i, mirror) for i in range(PIECES)]
@@ -108,14 +128,20 @@
     for copy in parked_copies:
         go(copy)
 
-    y = lax.div(section, 2)
-    near = jnp.logical_or(lax.rem(y, 4) == 0, lax.rem(y, 4) == 3)
-
     def send_forward(pieces, when):
         @pl.when(when)
         def _():
             for i in pieces:
                 forward_copies[i].start()
+
+    last = PIECES - 1
+    detour_in = remote(
+        fwd.at[:, piece(last)], stop, y_send.at[3 * PIECES], y_recv.at[3 * PIECES], stop_at
+    )
+    detour_out = remote(
+        stop, o_parked.at[:, piece(last)],
+        y_send.at[3 * PIECES + 1], y_recv.at[PIECES + last], stop_to,
+    )
 
     class Gather:
         def __init__(self, number, w, start, stop, x_first):
@@ -175,9 +201,6 @@
     up = Gather(1, 1, SPLIT, D, False)
     both = Gather(2, slice(None), 0, SPLIT, True)
 
-    def piece(i):
-        return pl.ds(i * PIECE, PIECE)
-
     def exchange(slot):
         return remote(
             pre_out.at[slot], pre_in.at[slot], m_send.at[slot], m_recv.at[slot], other
@@ -223,6 +246,7 @@
         cols = piece(i)
         chosen = lax.dot_general(chosen_t, vis[:, cols], TN, preferred_element_type=F32)
         fwd[:, cols] = jnp.where(hit > 0.5, chosen, sec[:, cols].astype(F32)).astype(BF16)
+    pl.when(detours)(detour_in.start)
 
     down.near1()
     up.start1()
@@ -258,10 +282,16 @@
     total = jnp.zeros((ROWS, R), F32)
     for i in range(PIECES):
         parked_copies[i].wait_recv()
-        send_forward([i], near)
+        if i < last:
+            send_forward([i], near)
         cols = piece(i)
         total += lax.dot_general(bwd[:, cols], weight(0, cols), NT, preferred_element_type=F32)
     send_partial(2, total)
+
+    @pl.when(stops)
+    def _():
+        detour_in.wait_recv()
+        detour_out.start()
 
     bwd_pre = summed(2)
     bwd_act = gelu(bwd_pre).astype(BF16)
@@ -387,22 +417,23 @@
     uz.stage_a()
     u1.stage_a()
     act[...] = gelu(summed(0)).astype(BF16)
+    outputs(0)
+    outputs(1)
     u0.stage_b()
-    send_forward(range(PIECES), jnp.logical_not(near))
     uz.stage_b()
     d0.stage_a()
-    outputs(0)
+    outputs(2)
+    outputs(3)
+    send_forward(range(last), far)
+    send_forward([last], jnp.logical_not(detours))
     dz.stage_a()
     u1.stage_b()
     u0.stage_c()
     uz.stage_c()
-    outputs(1)
     d1.stage_a()
-    outputs(2)
     d0.stage_b()
     u0.stage_d()
     uz.stage_d()
-    outputs(3)
     dz.stage_b()
     u1.stage_c()
     u1.stage_d()
@@ -426,8 +457,11 @@
 
     for copy in forward_copies + shift_copies:
         copy.wait_recv()
-    for copy in pending + forward_copies:
+    for copy in pending + forward_copies[:last]:
         copy.wait_send()
+    pl.when(jnp.logical_not(detours))(forward_copies[last].wait_send)
+    pl.when(detours)(detour_in.wait_send)
+    pl.when(stops)(detour_out.wait_send)
 
 
 def write_out(*refs):
@@ -465,6 +499,7 @@
             pltpu.VMEM((ROWS, R), BF16),
             pltpu.VMEM((R, ROWS), BF16),
             pltpu.VMEM((R, ROWS), BF16),
+            pltpu.VMEM((ROWS, PIECE), BF16),
             pltpu.VMEM((2, 2, SHARE, D), BF16),
             pltpu.VMEM((2, 2, SHARE, D), BF16),
             pltpu.VMEM((2, 4, SHARE, D), BF16),
@@ -481,8 +516,8 @@
             dma((6 * N_REDUCE,)),
             dma((3,)),
             dma((3,)),
-            dma((3 * PIECES,)),
-            dma((3 * PIECES,)),
+            dma((3 * PIECES + 2,)),
+            dma((3 * PIECES + 1,)),
         ],
         compiler_params=pltpu.CompilerParams(
             collective_id=0, has_side_effects=True, vmem_limit_bytes=40 * 2**20

time: 98.7 us -> 99.3 us (level)
  the two profiles are of different devices: /device:TPU:6 before, /device:TPU:64 now
where the time goes in v4:
time: 99.3 us; the launch traced here: 99.1 us
  Pallas kernels  98.5 us (99%)
    pallas_call x1, Pallas kernels, local(): pl.pallas_call(kernel, out_shape=(pltpu.VMEM((ROWS, D), BF16),) * 3 + (pl...  97 us

profile of v4, /device:TPU:64, one launch (start us, length us, event | category | flops | bytes accessed | tf_op | source)
XLA Modules:
  0.0 99.1 jit_solution(2813177004397795592)
XLA Ops:
  0.6 97.0 %relay_tick.1 = (bf16[104,3584]{1,0:T(8,128)(2,1)S(1)}, bf16[104,3584]{1,0:T(8,128)(2,1)S(1)}, bf16[104,3584]{1,0:T(8,128)(2,1)S(1)}, bf16[16,3584]{1,0:T(8,128)(2,1)S(1)}, bf16[16,3584]{1,0:T(8,128)(2,1)S(1)}) custom-call(bf16[104,3584]{1,0:T(8,128)(2,1)} %bitcast.11, bf16[24,3584]{1,0:T(8,128)(2,1)} %bitcast.17, s32[1,104]{1,0:T(1,128)} %alternate_ref.1, ...), custom_call_target="tpu_custom_call" | custom-call | flops 1335885824 | bytes 4472832 | tf_op jit(solution)/shard_map/relay_tick/pallas_call | solution.py:481
  97.7 1.5 %write_out.1 = (bf16[104,3584]{1,0:T(8,128)(2,1)}, bf16[104,3584]{1,0:T(8,128)(2,1)}, bf16[104,3584]{1,0:T(8,128)(2,1)}, bf16[16,3584]{1,0:T(8,128)(2,1)}, bf16[16,3584]{1,0:T(8,128)(2,1)}) custom-call(bf16[104,3584]{1,0:T(8,128)(2,1)S(1)} %get-tuple-element.15.refs_0_, bf16[104,3584]{1,0:T(8,128)(2,1)S(1)} %get-tuple-element.16.refs_1_, ...), custom_call_target="tpu_custom_call" | custom-call | tf_op jit(solution)/shard_map/write_out/pallas_call | solution.py:536

commit v5 on v4

--- a/solution.py
+++ b/solution.py
@@ -16,11 +16,12 @@
 ROWS = 104
 VISION = 24
 SHARE = 16
-TILE = 256
 PIECES = 4
 PIECE = D // PIECES
+HANDED = 2
+HAND = 3 * PIECES
 NX, NZ = 4, 4
-SPLIT = 3 * TILE
+SPLIT = 1024
 
 N_GATHER = 16
 N_REDUCE = 12
@@ -44,8 +45,8 @@
     section_ref, vision_ref, alternate_ref, grad_ref, parked_ref, wd_ref, wu_ref,
     o_section, o_parked, o_input_grad, o_up, o_down,
     sec, vis, alt, grad, fwd, bwd, out, weights, parts,
-    pre_out, pre_in, act, slope_act, act_t, grad_t,
-    stop, opp_up, opp_dn, from_up, from_dn, opp2_up, opp2_dn, from2_up, from2_dn, sums,
+    pre_out, pre_in, bwd_pre, act, slope_act, act_t, grad_t,
+    hand, stop, opp_up, opp_dn, from_up, from_dn, opp2_up, opp2_dn, from2_up, from2_dn, sums,
     local_sem, g_send, g_recv, r_send, r_recv, m_send, m_recv, y_send, y_recv,
 ):
     section = lax.axis_index("section")
@@ -96,6 +97,8 @@
     near = jnp.logical_or(turn == 0, turn == 3)
     far = jnp.logical_not(near)
     detours, stops, ends = turn == 2, turn == 0, turn == 1
+    next_chip = {"section": lax.rem(section + 2, 16)}
+    last_chip = {"section": lax.rem(section + 14, 16)}
     stop_at = {"section": lax.rem(section + 12, 16)}
     stop_from = {"section": lax.rem(section + 4, 16)}
     stop_to = {"section": lax.rem(y + 5, 8) * 2 + 1 - core}
@@ -111,8 +114,9 @@
     pl.when(detours)(lambda: greet(stop_at))
     pl.when(stops)(lambda: greet(stop_from, stop_to))
     pl.when(ends)(lambda: greet(end_from))
+    pl.when(core == 0)(lambda: greet(next_chip, last_chip))
     extra = jnp.where(stops, 2, jnp.where(turn == 3, 0, 1))
-    pl.semaphore_wait(barrier, 8 + extra)
+    pl.semaphore_wait(barrier, 8 + extra + 2 * (1 - core))
 
     def piece(i):
         return pl.ds(i * PIECE, PIECE)
@@ -133,6 +137,17 @@
         def _():
             for i in pieces:
                 forward_copies[i].start()
+
+    hand_copies, pass_copies = {}, {}
+    for i in range(HANDED, PIECES):
+        held = hand.at[:, pl.ds((i - HANDED) * PIECE, PIECE)]
+        hand_copies[i] = remote(
+            out.at[:, piece(i)], held, y_send.at[HAND + i], y_recv.at[HAND + i], preceding
+        )
+        pass_copies[i] = remote(
+            held, o_section.at[:, piece(i)],
+            y_send.at[HAND + i], y_recv.at[2 * PIECES + i], next_chip,
+        )
 
     last = PIECES - 1
     detour_in = remote(
@@ -170,25 +185,25 @@
             go(self.copy(4 + k, self.up2, a=k))
             go(self.copy(8 + k, self.dn2, a=k))
 
-        def near1(self):
-            self.copy(0, self.up).wait_recv()
-            go(self.copy(2, self.up, a=-1, cols=self.low))
-            self.start2(3)
-            self.copy(1, self.dn).wait_recv()
-            go(self.copy(3, self.dn, a=1, cols=self.high))
-            self.start2(1)
+        def near1(self, side):
+            self.copy(side, (self.up, self.dn)[side]).wait_recv()
+            if side == 0:
+                go(self.copy(2, self.up, a=-1, cols=self.low))
+                self.start2(3)
+            else:
+                go(self.copy(3, self.dn, a=1, cols=self.high))
+                self.start2(1)
 
         def far1(self):
             self.copy(2, self.up, cols=self.low).wait_recv()
             self.copy(3, self.dn, cols=self.high).wait_recv()
             self.start2(2)
 
-        def near2(self, k):
-            self.copy(4 + k, self.up2).wait_recv()
-            if k % 2 == 0:
+        def near2(self, k, side):
+            self.copy(4 + 4 * side + k, (self.up2, self.dn2)[side]).wait_recv()
+            if k % 2 == 0 and side == 0:
                 go(self.copy(12 + k // 2, self.up2, a=k, b=-1))
-            self.copy(8 + k, self.dn2).wait_recv()
-            if k % 2 == 1:
+            if k % 2 == 1 and side == 1:
                 go(self.copy(14 + k // 2, self.dn2, a=k, b=1))
 
         def far2(self, k):
@@ -233,6 +248,7 @@
     both.start1()
     both.start2(0)
     up.start2(0)
+    up.start1()
 
     for load in loads[:3]:
         load.wait()
@@ -248,63 +264,97 @@
         fwd[:, cols] = jnp.where(hit > 0.5, chosen, sec[:, cols].astype(F32)).astype(BF16)
     pl.when(detours)(detour_in.start)
 
-    down.near1()
-    up.start1()
-    both.near1()
-    down.near2(0)
+    def backward_rows():
+        total = jnp.zeros((ROWS, R), F32)
+        for i in range(PIECES):
+            parked_copies[i].wait_recv()
+            send_forward([i], near)
+            cols = piece(i)
+            total += lax.dot_general(
+                bwd[:, cols], weight(0, cols), NT, preferred_element_type=F32
+            )
+        send_partial(2, total)
+
+        @pl.when(stops)
+        def _():
+            detour_in.wait_recv()
+            detour_out.start()
+
+    both.near1(0)
+    both.near1(1)
+    down.near2(0, 0)
+    down.near2(0, 1)
+    up.near2(0, 0)
+    up.near2(0, 1)
     both.far1()
-    both.near2(0)
+    down.far2(0)
+    up.far2(0)
+    both.near2(0, 0)
+    both.near2(0, 1)
+    down.near1(0)
+    down.near1(1)
+    up.near1(1)
+    up.near1(0)
+    down.near2(3, 0)
+    down.near2(3, 1)
+    down.near2(1, 0)
+    down.near2(1, 1)
+    both.near2(3, 1)
+    both.near2(1, 1)
+    up.near2(1, 0)
+    up.near2(3, 0)
+    both.near2(2, 1)
+    both.near2(3, 0)
+    both.near2(1, 0)
+    up.near2(1, 1)
+    up.near2(3, 1)
     down.far1()
-    down.near2(3)
-    down.near2(1)
-    both.near2(3)
-    both.near2(1)
-    up.near1()
-    down.far2(0)
-    down.near2(2)
+    both.near2(2, 0)
     up.far1()
-    both.near2(2)
-    up.near2(0)
-    up.near2(3)
-    up.near2(1)
-    up.far2(0)
-    up.near2(2)
-    for k in (3, 1, 2):
-        down.far2(k)
-    for k in (0, 3, 1, 2):
-        both.far2(k)
-    partial(0, fwd, 0)
-    for k in (3, 1, 2):
-        up.far2(k)
+    down.far2(3)
+    both.far2(0)
+    down.far2(1)
+    down.near2(2, 0)
+    both.far2(3)
+    both.far2(1)
+    both.far2(2)
+    up.near2(2, 0)
+    up.far2(1)
+    down.far2(2)
+    up.far2(3)
+    down.near2(2, 1)
+    backward_rows()
+    up.near2(2, 1)
+    up.far2(2)
     loads[3].wait()
     partial(1, grad, 1)
-
-    total = jnp.zeros((ROWS, R), F32)
-    for i in range(PIECES):
-        parked_copies[i].wait_recv()
-        if i < last:
-            send_forward([i], near)
-        cols = piece(i)
-        total += lax.dot_general(bwd[:, cols], weight(0, cols), NT, preferred_element_type=F32)
-    send_partial(2, total)
-
-    @pl.when(stops)
-    def _():
-        detour_in.wait_recv()
-        detour_out.start()
-
-    bwd_pre = summed(2)
-    bwd_act = gelu(bwd_pre).astype(BF16)
-    act_t[...] = bwd_act.T
-    pre_grad = (summed(1) * gelu_slope(bwd_pre)).astype(BF16)
-    slope_act[...] = pre_grad
-    grad_t[...] = pre_grad.T
+    partial(0, fwd, 0)
+
+    def backward_act():
+        bwd_pre[...] = summed(2)
+        act_t[...] = gelu(bwd_pre[...]).astype(BF16).T
+
+    def slopes():
+        pre_grad = (summed(1) * gelu_slope(bwd_pre[...])).astype(BF16)
+        slope_act[...] = pre_grad
+        grad_t[...] = pre_grad.T
 
     def outputs(i):
         cols = piece(i)
         product = jnp.dot(act[...], weight(1, cols), preferred_element_type=F32)
         out[:, cols] = (fwd[:, cols].astype(F32) + product).astype(BF16)
-        go(shift_copies[i])
+        if i < HANDED:
+            go(shift_copies[i])
+        else:
+            pl.when(core == 0)(shift_copies[i].start)
+            pl.when(core == 1)(hand_copies[i].start)
+
+    def pass_on():
+        @pl.when(core == 0)
+        def _():
+            for i in range(HANDED, PIECES):
+                hand_copies[i].wait_recv()
+                pass_copies[i].start()
 
     def add_into(total, term):
         total[...] = (total[...].astype(F32) + term[...].astype(F32)).astype(BF16)
@@ -351,27 +401,30 @@
             index = self.base + m
             return remote(src, dst, r_send.at[index], r_recv.at[index], to)
 
-        def stage_a(self):
+        def send_far(self):
             lhs, rhs = ((act_t, grad), (grad_t, bwd))[self.w]
-
-            steps = max(1, (self.stop - self.start) // 640)
+            steps = -(-(self.stop - self.start) // 640)
             width = (self.stop - self.start) // steps
             for i in range(steps):
                 cols = pl.ds(self.start + i * width, width)
                 product = jnp.dot(lhs[...], rhs[:, cols], preferred_element_type=F32)
                 parts[self.w, :, :, :, cols] = product.astype(BF16).reshape(NX, NZ, SHARE, width)
-            for m in range(4):
-                go(self.copy(m))
-
-        def stage_b(self):
-            self.copy(0).wait_recv()
-            add_into(self.block(-1, 0, 2), self.term(opp_up, 0, 2))
-            go(self.copy(4))
-            self.copy(1).wait_recv()
-            add_into(self.block(1, 2, 2), self.term(opp_dn, 0, 2))
-            go(self.copy(5))
-
-        def stage_c(self):
+            go(self.copy(0))
+            go(self.copy(1))
+
+        def send_near(self):
+            go(self.copy(2))
+            go(self.copy(3))
+
+        def relay(self, side):
+            self.copy(side).wait_recv()
+            if side == 0:
+                add_into(self.block(-1, 0, 2), self.term(opp_up, 0, 2))
+            else:
+                add_into(self.block(1, 2, 2), self.term(opp_dn, 0, 2))
+            go(self.copy(4 + side))
+
+        def fold(self):
             for m in (2, 3, 4, 5):
                 self.copy(m).wait_recv()
             self.term(sums, 0, 4)[...] = (
@@ -382,16 +435,16 @@
             for m in (6, 7, 8, 9):
                 go(self.copy(m))
 
-        def stage_d(self):
+        def relay2(self, side):
             w = self.w
-            self.copy(6).wait_recv()
-            add_into(self.total(-1, self.low), opp2_up.at[w, :, self.low])
-            go(self.copy(10))
-            self.copy(7).wait_recv()
-            add_into(self.total(1, self.high), opp2_dn.at[w, :, self.high])
-            go(self.copy(11))
-
-        def stage_e(self):
+            self.copy(6 + side).wait_recv()
+            if side == 0:
+                add_into(self.total(-1, self.low), opp2_up.at[w, :, self.low])
+            else:
+                add_into(self.total(1, self.high), opp2_dn.at[w, :, self.high])
+            go(self.copy(10 + side))
+
+        def finish(self):
             w, cols = self.w, self.all
             for m in (8, 9, 10, 11):
                 self.copy(m).wait_recv()
@@ -409,51 +462,72 @@
         product = jnp.dot(slope_act[...], weight(0, cols), preferred_element_type=F32)
         o_input_grad[:, cols] = (grad[:, cols].astype(F32) + product).astype(BF16)
 
-    cut = SPLIT + 6 * TILE
+    cut = (SPLIT + D) // 2
     u0, u1 = Reduce(0, 0, SPLIT, cut, True), Reduce(1, 0, cut, D, True)
     d0, d1 = Reduce(2, 1, SPLIT, cut, True), Reduce(3, 1, cut, D, True)
     uz, dz = Reduce(4, 0, 0, SPLIT, False), Reduce(5, 1, 0, SPLIT, False)
-    u0.stage_a()
-    uz.stage_a()
-    u1.stage_a()
+    backward_act()
+    u0.send_far()
+    slopes()
+    u0.send_near()
+    uz.send_far()
+    u1.send_far()
+    uz.send_near()
+    u1.send_near()
+    dz.send_far()
+    d0.send_far()
+    u0.relay(0)
+    u0.relay(1)
+    dz.send_near()
+    d0.send_near()
+    d1.send_far()
+    d1.send_near()
     act[...] = gelu(summed(0)).astype(BF16)
     outputs(0)
     outputs(1)
-    u0.stage_b()
-    uz.stage_b()
-    d0.stage_a()
     outputs(2)
     outputs(3)
     send_forward(range(last), far)
-    send_forward([last], jnp.logical_not(detours))
-    dz.stage_a()
-    u1.stage_b()
-    u0.stage_c()
-    uz.stage_c()
-    d1.stage_a()
-    d0.stage_b()
-    u0.stage_d()
-    uz.stage_d()
-    dz.stage_b()
-    u1.stage_c()
-    u1.stage_d()
-    dz.stage_c()
+    send_forward([last], ends)
+    uz.relay(0)
+    uz.relay(1)
     input_grad(0)
     input_grad(1)
-    d1.stage_b()
-    d0.stage_c()
-    u0.stage_e()
-    uz.stage_e()
-    dz.stage_d()
-    d0.stage_d()
-    u1.stage_e()
     input_grad(2)
     input_grad(3)
-    d1.stage_c()
-    d1.stage_d()
-    dz.stage_e()
-    d0.stage_e()
-    d1.stage_e()
+    pass_on()
+    u1.relay(1)
+    u1.relay(0)
+    dz.relay(0)
+    dz.relay(1)
+    d0.relay(0)
+    d0.relay(1)
+    u0.fold()
+    uz.fold()
+    d1.relay(0)
+    d1.relay(1)
+    u1.fold()
+    uz.relay2(1)
+    uz.relay2(0)
+    u0.relay2(0)
+    u0.relay2(1)
+    dz.fold()
+    d0.fold()
+    uz.finish()
+    u1.relay2(0)
+    u1.relay2(1)
+    d1.fold()
+    dz.relay2(0)
+    dz.relay2(1)
+    u0.finish()
+    d0.relay2(1)
+    d0.relay2(0)
+    dz.finish()
+    u1.finish()
+    d1.relay2(0)
+    d1.relay2(1)
+    d0.finish()
+    d1.finish()
 
     for copy in forward_copies + shift_copies:
         copy.wait_recv()
@@ -461,6 +535,10 @@
         copy.wait_send()
     pl.when(jnp.logical_not(detours))(forward_copies[last].wait_send)
     pl.when(detours)(detour_in.wait_send)
+    for i in range(HANDED, PIECES):
+        pl.when(core == 0)(shift_copies[i].wait_send)
+        pl.when(core == 0)(pass_copies[i].wait_send)
+        pl.when(core == 1)(hand_copies[i].wait_send)
     pl.when(stops)(detour_out.wait_send)
 
 
@@ -495,10 +573,12 @@
             pltpu.VMEM((2, NX, NZ, SHARE, D), BF16),
             pltpu.VMEM((3, ROWS, R), BF16),
             pltpu.VMEM((3, ROWS, R), BF16),
+            pltpu.VMEM((ROWS, R), F32),
             pltpu.VMEM((ROWS, R), BF16),
             pltpu.VMEM((ROWS, R), BF16),
             pltpu.VMEM((R, ROWS), BF16),
             pltpu.VMEM((R, ROWS), BF16),
+            pltpu.VMEM((ROWS, (PIECES - HANDED) * PIECE), BF16),
             pltpu.VMEM((ROWS, PIECE), BF16),
             pltpu.VMEM((2, 2, SHARE, D), BF16),
             pltpu.VMEM((2, 2, SHARE, D), BF16),
@@ -516,8 +596,8 @@
             dma((6 * N_REDUCE,)),
             dma((3,)),
             dma((3,)),
-            dma((3 * PIECES + 2,)),
-            dma((3 * PIECES + 1,)),
+            dma((4 * PIECES,)),
+            dma((4 * PIECES,)),
         ],
         compiler_params=pltpu.CompilerParams(
             collective_id=0, has_side_effects=True, vmem_limit_bytes=40 * 2**20

time: 99.3 us -> 94 us (0.947)
  the two profiles are of different devices: /device:TPU:64 before, /device:TPU:6 now
where the time goes in v5:
time: 94 us; the launch traced here: 92.3 us
  Pallas kernels  91.7 us (98%)
    pallas_call x1, Pallas kernels, local(): pl.pallas_call(kernel, out_shape=(pltpu.VMEM((ROWS, D), BF16),) * 3 + (pl...  90.2 us

profile of v5, /device:TPU:6, one launch (start us, length us, event | category | flops | bytes accessed | tf_op | source)
XLA Modules:
  0.0 92.3 jit_solution(4463539935723865224)
XLA Ops:
  0.6 90.2 %relay_tick.1 = (bf16[104,3584]{1,0:T(8,128)(2,1)S(1)}, bf16[104,3584]{1,0:T(8,128)(2,1)S(1)}, bf16[104,3584]{1,0:T(8,128)(2,1)S(1)}, bf16[16,3584]{1,0:T(8,128)(2,1)S(1)}, bf16[16,3584]{1,0:T(8,128)(2,1)S(1)}) custom-call(bf16[104,3584]{1,0:T(8,128)(2,1)} %bitcast.11, bf16[24,3584]{1,0:T(8,128)(2,1)} %bitcast.17, s32[1,104]{1,0:T(1,128)} %alternate_ref.1, ...), custom_call_target="tpu_custom_call" | custom-call | flops 1335885824 | bytes 4472832 | tf_op jit(solution)/shard_map/relay_tick/pallas_call | solution.py:559
  90.9 1.5 %write_out.1 = (bf16[104,3584]{1,0:T(8,128)(2,1)}, bf16[104,3584]{1,0:T(8,128)(2,1)}, bf16[104,3584]{1,0:T(8,128)(2,1)}, bf16[16,3584]{1,0:T(8,128)(2,1)}, bf16[16,3584]{1,0:T(8,128)(2,1)}) custom-call(bf16[104,3584]{1,0:T(8,128)(2,1)S(1)} %get-tuple-element.15.refs_0_, bf16[104,3584]{1,0:T(8,128)(2,1)S(1)} %get-tuple-element.16.refs_1_, ...), custom_call_target="tpu_custom_call" | custom-call | tf_op jit(solution)/shard_map/write_out/pallas_call | solution.py:616

commit v6 on v5

--- a/solution.py
+++ b/solution.py
@@ -18,6 +18,7 @@
 SHARE = 16
 PIECES = 4
 PIECE = D // PIECES
+CUT = 512
 HANDED = 2
 HAND = 3 * PIECES
 NX, NZ = 4, 4
@@ -45,9 +46,10 @@
     section_ref, vision_ref, alternate_ref, grad_ref, parked_ref, wd_ref, wu_ref,
     o_section, o_parked, o_input_grad, o_up, o_down,
     sec, vis, alt, grad, fwd, bwd, out, weights, parts,
-    pre_out, pre_in, bwd_pre, act, slope_act, act_t, grad_t,
+    pre_out, pre_in, bwd_pre, act, slope_act, act_ts, grad_t, grads, by_right, by_left,
     hand, stop, opp_up, opp_dn, from_up, from_dn, opp2_up, opp2_dn, from2_up, from2_dn, sums,
-    local_sem, g_send, g_recv, r_send, r_recv, m_send, m_recv, y_send, y_recv,
+    u_parts, u_opp_up, u_opp_dn, u_from_up, u_from_dn, ready,
+    local_sem, g_send, g_recv, r_send, r_recv, m_send, m_recv, y_send, y_recv, x_send, x_recv,
 ):
     section = lax.axis_index("section")
     dp = lax.axis_index("dp")
@@ -65,6 +67,7 @@
     preceding = {"section": lax.rem(section + 15, 16)}
     other = {"mp": 1 - mp}
     right, left = {"dp": chunk(x + 1, z)}, {"dp": chunk(x - 1, z)}
+    opposite = {"dp": chunk(x + 2, z)}
     plus, minus = {"dp": chunk(x, z + 1)}, {"dp": chunk(x, z - 1)}
 
     pending = []
@@ -110,13 +113,13 @@
         for partner in partners:
             pl.semaphore_signal(barrier, inc=1, device_id=partner, device_id_type=MESH)
 
-    greet(mirror, following, preceding, other, right, left, plus, minus)
+    greet(mirror, following, preceding, other, right, left, opposite, plus, minus)
     pl.when(detours)(lambda: greet(stop_at))
     pl.when(stops)(lambda: greet(stop_from, stop_to))
     pl.when(ends)(lambda: greet(end_from))
     pl.when(core == 0)(lambda: greet(next_chip, last_chip))
     extra = jnp.where(stops, 2, jnp.where(turn == 3, 0, 1))
-    pl.semaphore_wait(barrier, 8 + extra + 2 * (1 - core))
+    pl.semaphore_wait(barrier, 9 + extra + 2 * (1 - core))
 
     def piece(i):
         return pl.ds(i * PIECE, PIECE)
@@ -243,26 +246,87 @@
 
     for load in loads[4:]:
         load.wait()
-    down.start1()
-    down.start2(0)
-    both.start1()
-    both.start2(0)
-    up.start2(0)
-    up.start1()
-
-    for load in loads[:3]:
-        load.wait()
-    picks = jnp.where(section == 0, alt[...], -1)
-    chosen_t = (lax.broadcasted_iota(jnp.int32, (VISION, ROWS), 0) == picks).astype(BF16)
-    hit = lax.dot_general(
-        chosen_t, jnp.ones((VISION, PIECE), BF16), TN, preferred_element_type=F32
-    )
-
-    for i in range(PIECES):
-        cols = piece(i)
-        chosen = lax.dot_general(chosen_t, vis[:, cols], TN, preferred_element_type=F32)
-        fwd[:, cols] = jnp.where(hit > 0.5, chosen, sec[:, cols].astype(F32)).astype(BF16)
-    pl.when(detours)(detour_in.start)
+    def choose_rows():
+        for load in loads[:3]:
+            load.wait()
+        picks = jnp.where(section == 0, alt[...], -1)
+        chosen_t = (lax.broadcasted_iota(jnp.int32, (VISION, ROWS), 0) == picks).astype(BF16)
+        hit = lax.dot_general(
+            chosen_t, jnp.ones((VISION, PIECE), BF16), TN, preferred_element_type=F32
+        )
+
+        for i in range(PIECES):
+            cols = piece(i)
+            chosen = lax.dot_general(chosen_t, vis[:, cols], TN, preferred_element_type=F32)
+            fwd[:, cols] = jnp.where(hit > 0.5, chosen, sec[:, cols].astype(F32)).astype(BF16)
+        pl.when(detours)(detour_in.start)
+
+        def backward_rows():
+            total = jnp.zeros((ROWS, R), F32)
+            for i in range(PIECES):
+                parked_copies[i].wait_recv()
+                send_forward([i], near)
+                cols = piece(i)
+                total += lax.dot_general(
+                    bwd[:, cols], weight(0, cols), NT, preferred_element_type=F32
+                )
+            send_partial(2, total)
+
+            @pl.when(stops)
+            def _():
+                detour_in.wait_recv()
+                detour_out.start()
+
+    def quarter(k, first=0, size=PIECE):
+        return pl.ds(pl.multiple_of(at(x + k, NX) * PIECE + first, 128), size)
+
+    def x_copy(m, src, dst, to):
+        return remote(src, dst, x_send.at[m], x_recv.at[m], to)
+
+    lows, highs = pl.ds(0, CUT), pl.ds(CUT, PIECE - CUT)
+    from_x = [at(x + k, NX) for k in range(-1, 2)]
+    row_copies = [
+        x_copy(0, grad.at[:, quarter(1)], grads.at[x], right),
+        x_copy(1, grad.at[:, quarter(-1)], grads.at[x], left),
+        x_copy(2, grad.at[:, quarter(2, 0, CUT)], by_right, right),
+        x_copy(3, grad.at[:, quarter(2, CUT, PIECE - CUT)], by_left, left),
+        x_copy(4, by_right, grads.at[from_x[0], :, lows], right),
+        x_copy(5, by_left, grads.at[from_x[2], :, highs], left),
+    ]
+    act_copies = [
+        x_copy(6, act_ts.at[x], act_ts.at[x], right),
+        x_copy(7, act_ts.at[x], act_ts.at[x], left),
+        x_copy(8, act_ts.at[from_x[0]], act_ts.at[from_x[0]], right),
+    ]
+
+    def rows_far():
+        go(row_copies[2])
+        go(row_copies[3])
+
+    def rows_near():
+        go(row_copies[0])
+        go(row_copies[1])
+        grads[x] = grad[:, quarter(0)]
+
+    def rows_relay(side):
+        row_copies[2 + side].wait_recv()
+        go(row_copies[4 + side])
+
+    def rows_done():
+        for m in (0, 1, 4, 5):
+            row_copies[m].wait_recv()
+
+    def act_send():
+        go(act_copies[0])
+        go(act_copies[1])
+
+    def act_relay():
+        act_copies[0].wait_recv()
+        go(act_copies[2])
+
+    def act_done():
+        act_copies[1].wait_recv()
+        act_copies[2].wait_recv()
 
     def backward_rows():
         total = jnp.zeros((ROWS, R), F32)
@@ -280,59 +344,9 @@
             detour_in.wait_recv()
             detour_out.start()
 
-    both.near1(0)
-    both.near1(1)
-    down.near2(0, 0)
-    down.near2(0, 1)
-    up.near2(0, 0)
-    up.near2(0, 1)
-    both.far1()
-    down.far2(0)
-    up.far2(0)
-    both.near2(0, 0)
-    both.near2(0, 1)
-    down.near1(0)
-    down.near1(1)
-    up.near1(1)
-    up.near1(0)
-    down.near2(3, 0)
-    down.near2(3, 1)
-    down.near2(1, 0)
-    down.near2(1, 1)
-    both.near2(3, 1)
-    both.near2(1, 1)
-    up.near2(1, 0)
-    up.near2(3, 0)
-    both.near2(2, 1)
-    both.near2(3, 0)
-    both.near2(1, 0)
-    up.near2(1, 1)
-    up.near2(3, 1)
-    down.far1()
-    both.near2(2, 0)
-    up.far1()
-    down.far2(3)
-    both.far2(0)
-    down.far2(1)
-    down.near2(2, 0)
-    both.far2(3)
-    both.far2(1)
-    both.far2(2)
-    up.near2(2, 0)
-    up.far2(1)
-    down.far2(2)
-    up.far2(3)
-    down.near2(2, 1)
-    backward_rows()
-    up.near2(2, 1)
-    up.far2(2)
-    loads[3].wait()
-    partial(1, grad, 1)
-    partial(0, fwd, 0)
-
     def backward_act():
         bwd_pre[...] = summed(2)
-        act_t[...] = gelu(bwd_pre[...]).astype(BF16).T
+        act_ts[x] = gelu(bwd_pre[...]).astype(BF16).T
 
     def slopes():
         pre_grad = (summed(1) * gelu_slope(bwd_pre[...])).astype(BF16)
@@ -360,8 +374,9 @@
         total[...] = (total[...].astype(F32) + term[...].astype(F32)).astype(BF16)
 
     class Reduce:
-        def __init__(self, number, w, start, stop, x_first):
-            self.base, self.w, self.start, self.stop = number * N_REDUCE, w, start, stop
+        def __init__(self, number, place, start, stop, x_first):
+            self.base, self.start, self.stop = number * N_REDUCE, start, stop
+            self.parts, self.opp_up, self.opp_dn, self.from_up, self.from_dn = place
             self.x_first = x_first
             self.a, self.b = (x, z) if x_first else (z, x)
             xs, zs = (right, left), (plus, minus)
@@ -373,42 +388,43 @@
         def block(self, a, b0, count):
             a = at(self.a + a, 4)
             if self.x_first:
-                return parts.at[self.w, a, pl.ds(b0, count), :, self.all]
-            return parts.at[self.w, pl.ds(b0, count), a, :, self.all]
+                return self.parts.at[a, pl.ds(b0, count), :, self.all]
+            return self.parts.at[pl.ds(b0, count), a, :, self.all]
 
         def term(self, ref, b0, count):
-            return ref.at[self.w, pl.ds(b0, count), :, self.all]
+            return ref.at[pl.ds(b0, count), :, self.all]
 
         def total(self, b, cols):
-            return sums.at[self.w, at(self.b + b, 4), :, cols]
+            return sums.at[at(self.b + b, 4), :, cols]
 
         def copy(self, m):
-            w = self.w
             src, dst, to = (
-                lambda: (self.block(2, 0, 2), self.term(opp_up, 0, 2), self.dn),
-                lambda: (self.block(2, 2, 2), self.term(opp_dn, 0, 2), self.up),
-                lambda: (self.block(-1, 2, 2), self.term(from_up, 2, 2), self.dn),
-                lambda: (self.block(1, 0, 2), self.term(from_dn, 0, 2), self.up),
-                lambda: (self.block(-1, 0, 2), self.term(from_up, 0, 2), self.dn),
-                lambda: (self.block(1, 2, 2), self.term(from_dn, 2, 2), self.up),
-                lambda: (self.total(2, self.low), opp2_up.at[w, :, self.low], self.dn2),
-                lambda: (self.total(2, self.high), opp2_dn.at[w, :, self.high], self.up2),
-                lambda: (self.total(-1, self.high), from2_up.at[w, :, self.high], self.dn2),
-                lambda: (self.total(1, self.low), from2_dn.at[w, :, self.low], self.up2),
-                lambda: (self.total(-1, self.low), from2_up.at[w, :, self.low], self.dn2),
-                lambda: (self.total(1, self.high), from2_dn.at[w, :, self.high], self.up2),
+                lambda: (self.block(2, 0, 2), self.term(self.opp_up, 0, 2), self.dn),
+                lambda: (self.block(2, 2, 2), self.term(self.opp_dn, 0, 2), self.up),
+                lambda: (self.block(-1, 2, 2), self.term(self.from_up, 2, 2), self.dn),
+                lambda: (self.block(1, 0, 2), self.term(self.from_dn, 0, 2), self.up),
+                lambda: (self.block(-1, 0, 2), self.term(self.from_up, 0, 2), self.dn),
+                lambda: (self.block(1, 2, 2), self.term(self.from_dn, 2, 2), self.up),
+                lambda: (self.total(2, self.low), opp2_up.at[:, self.low], self.dn2),
+                lambda: (self.total(2, self.high), opp2_dn.at[:, self.high], self.up2),
+                lambda: (self.total(-1, self.high), from2_up.at[:, self.high], self.dn2),
+                lambda: (self.total(1, self.low), from2_dn.at[:, self.low], self.up2),
+                lambda: (self.total(-1, self.low), from2_up.at[:, self.low], self.dn2),
+                lambda: (self.total(1, self.high), from2_dn.at[:, self.high], self.up2),
             )[m]()
+            return self.message(m, src, dst, to)
+
+        def message(self, m, src, dst, to):
             index = self.base + m
             return remote(src, dst, r_send.at[index], r_recv.at[index], to)
 
         def send_far(self):
-            lhs, rhs = ((act_t, grad), (grad_t, bwd))[self.w]
             steps = -(-(self.stop - self.start) // 640)
             width = (self.stop - self.start) // steps
             for i in range(steps):
                 cols = pl.ds(self.start + i * width, width)
-                product = jnp.dot(lhs[...], rhs[:, cols], preferred_element_type=F32)
-                parts[self.w, :, :, :, cols] = product.astype(BF16).reshape(NX, NZ, SHARE, width)
+                product = jnp.dot(grad_t[...], bwd[:, cols], preferred_element_type=F32)
+                parts[:, :, :, cols] = product.astype(BF16).reshape(NX, NZ, SHARE, width)
             go(self.copy(0))
             go(self.copy(1))
 
@@ -419,114 +435,190 @@
         def relay(self, side):
             self.copy(side).wait_recv()
             if side == 0:
-                add_into(self.block(-1, 0, 2), self.term(opp_up, 0, 2))
+                add_into(self.block(-1, 0, 2), self.term(self.opp_up, 0, 2))
             else:
-                add_into(self.block(1, 2, 2), self.term(opp_dn, 0, 2))
+                add_into(self.block(1, 2, 2), self.term(self.opp_dn, 0, 2))
             go(self.copy(4 + side))
 
-        def fold(self):
+        def folded(self):
             for m in (2, 3, 4, 5):
                 self.copy(m).wait_recv()
-            self.term(sums, 0, 4)[...] = (
+            return (
                 self.block(0, 0, 4)[...].astype(F32)
-                + self.term(from_up, 0, 4)[...].astype(F32)
-                + self.term(from_dn, 0, 4)[...].astype(F32)
-            ).astype(BF16)
+                + self.term(self.from_up, 0, 4)[...].astype(F32)
+                + self.term(self.from_dn, 0, 4)[...].astype(F32)
+            )
+
+        def fold(self):
+            self.term(sums, 0, 4)[...] = self.folded().astype(BF16)
             for m in (6, 7, 8, 9):
                 go(self.copy(m))
 
         def relay2(self, side):
-            w = self.w
             self.copy(6 + side).wait_recv()
             if side == 0:
-                add_into(self.total(-1, self.low), opp2_up.at[w, :, self.low])
+                add_into(self.total(-1, self.low), opp2_up.at[:, self.low])
             else:
-                add_into(self.total(1, self.high), opp2_dn.at[w, :, self.high])
+                add_into(self.total(1, self.high), opp2_dn.at[:, self.high])
             go(self.copy(10 + side))
 
         def finish(self):
-            w, cols = self.w, self.all
+            cols = self.all
             for m in (8, 9, 10, 11):
                 self.copy(m).wait_recv()
             total = (
-                parts[w, x, z, :, cols].astype(F32)
-                + from_up[w, self.b, :, cols].astype(F32)
-                + from_dn[w, self.b, :, cols].astype(F32)
-                + from2_up[w, :, cols].astype(F32)
-                + from2_dn[w, :, cols].astype(F32)
+                parts[x, z, :, cols].astype(F32)
+                + from_up[self.b, :, cols].astype(F32)
+                + from_dn[self.b, :, cols].astype(F32)
+                + from2_up[:, cols].astype(F32)
+                + from2_dn[:, cols].astype(F32)
             )
-            (o_up, o_down)[w][:, cols] = (total * (1.0 / 16)).astype(BF16)
+            o_down[:, cols] = (total * (1.0 / 16)).astype(BF16)
+
+    class ReduceUp(Reduce):
+        def send_far(self):
+            for cols in (lows, highs):
+                product = jnp.zeros((R, cols.size), F32)
+                for i in range(NX):
+                    product += jnp.dot(
+                        act_ts[i], grads[i, :, cols], preferred_element_type=F32
+                    )
+                u_parts[:, :, :, cols] = product.astype(BF16).reshape(NX, NZ, SHARE, cols.size)
+            go(self.copy(0))
+            go(self.copy(1))
+
+        def owner(self, m):
+            k, to = ((1, right), (-1, left), (2, opposite))[m]
+            return self.message(6 + m, ready.at[at(x + k, NX)], o_up.at[:, quarter(0)], to)
+
+        def fold(self):
+            ready[...] = (self.folded() * (1.0 / 16)).astype(BF16)
+            for m in (2, 0, 1):
+                go(self.owner(m))
+            o_up[:, quarter(0)] = ready[x]
+
+        def finish(self):
+            for m in range(3):
+                self.owner(m).wait_recv()
 
     def input_grad(i):
         cols = piece(i)
         product = jnp.dot(slope_act[...], weight(0, cols), preferred_element_type=F32)
         o_input_grad[:, cols] = (grad[:, cols].astype(F32) + product).astype(BF16)
 
-    cut = (SPLIT + D) // 2
-    u0, u1 = Reduce(0, 0, SPLIT, cut, True), Reduce(1, 0, cut, D, True)
-    d0, d1 = Reduce(2, 1, SPLIT, cut, True), Reduce(3, 1, cut, D, True)
-    uz, dz = Reduce(4, 0, 0, SPLIT, False), Reduce(5, 1, 0, SPLIT, False)
+    down_place = (parts, opp_up, opp_dn, from_up, from_dn)
+    up_place = (u_parts, u_opp_up, u_opp_dn, u_from_up, u_from_dn)
+    d0, d1 = Reduce(0, down_place, 512, 2048, True), Reduce(1, down_place, 2048, D, True)
+    dz = Reduce(2, down_place, 0, 512, False)
+    u0 = ReduceUp(3, up_place, 0, PIECE, False)
+
+    both.start1()
+    down.start2(0)
+    down.start1()
+    up.start2(0)
+    both.start2(0)
+    up.start1()
+    loads[3].wait()
+    rows_far()
+    rows_near()
+    choose_rows()
+    both.near1(0)
+    both.near1(1)
+    down.near2(0, 0)
+    down.near2(0, 1)
+    up.near2(0, 0)
+    up.near2(0, 1)
+    rows_relay(1)
+    both.far1()
+    both.near2(0, 0)
+    both.near2(0, 1)
+    rows_relay(0)
+    down.near1(0)
+    down.near1(1)
+    up.near1(1)
+    up.near1(0)
+    down.far2(0)
+    down.near2(3, 1)
+    up.far2(0)
+    down.near2(1, 1)
+    both.near2(3, 1)
+    both.near2(1, 1)
+    up.near2(1, 1)
+    up.near2(3, 1)
+    both.near2(3, 0)
+    both.near2(1, 0)
+    both.near2(2, 1)
+    down.far1()
+    down.near2(3, 0)
+    down.near2(1, 0)
+    up.far1()
+    rows_done()
+    up.near2(1, 0)
+    up.near2(3, 0)
+    both.near2(2, 0)
+    both.far2(0)
+    down.far2(3)
+    down.far2(1)
+    down.near2(2, 0)
+    both.far2(3)
+    both.far2(1)
+    up.near2(2, 0)
+    both.far2(2)
+    up.far2(1)
+    up.far2(3)
+    down.near2(2, 1)
+    up.near2(2, 1)
+    down.far2(2)
+    backward_rows()
+    partial(0, fwd, 0)
+    up.far2(2)
+    partial(1, grad, 1)
     backward_act()
-    u0.send_far()
-    slopes()
-    u0.send_near()
-    uz.send_far()
-    u1.send_far()
-    uz.send_near()
-    u1.send_near()
-    dz.send_far()
-    d0.send_far()
-    u0.relay(0)
-    u0.relay(1)
-    dz.send_near()
-    d0.send_near()
-    d1.send_far()
-    d1.send_near()
+    act_send()
     act[...] = gelu(summed(0)).astype(BF16)
     outputs(0)
     outputs(1)
     outputs(2)
+    slopes()
+    dz.send_far()
+    act_relay()
+    dz.send_near()
+    d0.send_far()
+    d1.send_far()
+    d0.send_near()
+    d1.send_near()
     outputs(3)
     send_forward(range(last), far)
     send_forward([last], ends)
-    uz.relay(0)
-    uz.relay(1)
+    act_done()
+    u0.send_far()
+    dz.relay(1)
+    dz.relay(0)
+    u0.send_near()
     input_grad(0)
     input_grad(1)
+    pass_on()
     input_grad(2)
+    d0.relay(0)
     input_grad(3)
-    pass_on()
-    u1.relay(1)
-    u1.relay(0)
-    dz.relay(0)
-    dz.relay(1)
-    d0.relay(0)
     d0.relay(1)
-    u0.fold()
-    uz.fold()
+    d1.relay(1)
     d1.relay(0)
-    d1.relay(1)
-    u1.fold()
-    uz.relay2(1)
-    uz.relay2(0)
-    u0.relay2(0)
-    u0.relay2(1)
     dz.fold()
+    u0.relay(0)
+    u0.relay(1)
     d0.fold()
-    uz.finish()
-    u1.relay2(0)
-    u1.relay2(1)
-    d1.fold()
     dz.relay2(0)
     dz.relay2(1)
-    u0.finish()
+    d1.fold()
+    dz.finish()
+    d0.relay2(0)
     d0.relay2(1)
-    d0.relay2(0)
-    dz.finish()
-    u1.finish()
+    u0.fold()
     d1.relay2(0)
     d1.relay2(1)
     d0.finish()
+    u0.finish()
     d1.finish()
 
     for copy in forward_copies + shift_copies:
@@ -570,34 +662,45 @@
             pltpu.VMEM((ROWS, D), BF16),
             pltpu.VMEM((ROWS, D), BF16),
             pltpu.VMEM((2, NX, NZ, SHARE, D), BF16),
-            pltpu.VMEM((2, NX, NZ, SHARE, D), BF16),
+            pltpu.VMEM((NX, NZ, SHARE, D), BF16),
             pltpu.VMEM((3, ROWS, R), BF16),
             pltpu.VMEM((3, ROWS, R), BF16),
             pltpu.VMEM((ROWS, R), F32),
             pltpu.VMEM((ROWS, R), BF16),
             pltpu.VMEM((ROWS, R), BF16),
+            pltpu.VMEM((NX, R, ROWS), BF16),
             pltpu.VMEM((R, ROWS), BF16),
-            pltpu.VMEM((R, ROWS), BF16),
+            pltpu.VMEM((NX, ROWS, PIECE), BF16),
+            pltpu.VMEM((ROWS, CUT), BF16),
+            pltpu.VMEM((ROWS, PIECE - CUT), BF16),
             pltpu.VMEM((ROWS, (PIECES - HANDED) * PIECE), BF16),
             pltpu.VMEM((ROWS, PIECE), BF16),
-            pltpu.VMEM((2, 2, SHARE, D), BF16),
-            pltpu.VMEM((2, 2, SHARE, D), BF16),
-            pltpu.VMEM((2, 4, SHARE, D), BF16),
-            pltpu.VMEM((2, 4, SHARE, D), BF16),
             pltpu.VMEM((2, SHARE, D), BF16),
             pltpu.VMEM((2, SHARE, D), BF16),
-            pltpu.VMEM((2, SHARE, D), BF16),
-            pltpu.VMEM((2, SHARE, D), BF16),
-            pltpu.VMEM((2, 4, SHARE, D), BF16),
+            pltpu.VMEM((4, SHARE, D), BF16),
+            pltpu.VMEM((4, SHARE, D), BF16),
+            pltpu.VMEM((SHARE, D), BF16),
+            pltpu.VMEM((SHARE, D), BF16),
+            pltpu.VMEM((SHARE, D), BF16),
+            pltpu.VMEM((SHARE, D), BF16),
+            pltpu.VMEM((4, SHARE, D), BF16),
+            pltpu.VMEM((NX, NZ, SHARE, PIECE), BF16),
+            pltpu.VMEM((2, SHARE, PIECE), BF16),
+            pltpu.VMEM((2, SHARE, PIECE), BF16),
+            pltpu.VMEM((4, SHARE, PIECE), BF16),
+            pltpu.VMEM((4, SHARE, PIECE), BF16),
+            pltpu.VMEM((4, SHARE, PIECE), BF16),
             dma((6,)),
             dma((3 * N_GATHER,)),
             dma((3 * N_GATHER,)),
-            dma((6 * N_REDUCE,)),
-            dma((6 * N_REDUCE,)),
+            dma((4 * N_REDUCE,)),
+            dma((4 * N_REDUCE,)),
             dma((3,)),
             dma((3,)),
             dma((4 * PIECES,)),
             dma((4 * PIECES,)),
+            dma((9,)),
+            dma((9,)),
         ],
         compiler_params=pltpu.CompilerParams(
             collective_id=0, has_side_effects=True, vmem_limit_bytes=40 * 2**20

time: 94 us -> 90.5 us (0.963)
  the two profiles are of different devices: /device:TPU:6 before, /device:TPU:9 now
where the time goes in v6:
time: 90.5 us; the launch traced here: 90.4 us
  Pallas kernels  89.7 us (99%)
    pallas_call x1, Pallas kernels, local(): pl.pallas_call(kernel, out_shape=(pltpu.VMEM((ROWS, D), BF16),) * 3 + (pl...  88.3 us

profile of v6, /device:TPU:9, one launch (start us, length us, event | category | flops | bytes accessed | tf_op | source)
XLA Modules:
  0.0 90.4 jit_solution(3020045405322319272)
XLA Ops:
  0.6 88.3 %relay_tick.1 = (bf16[104,3584]{1,0:T(8,128)(2,1)S(1)}, bf16[104,3584]{1,0:T(8,128)(2,1)S(1)}, bf16[104,3584]{1,0:T(8,128)(2,1)S(1)}, bf16[16,3584]{1,0:T(8,128)(2,1)S(1)}, bf16[16,3584]{1,0:T(8,128)(2,1)S(1)}) custom-call(bf16[104,3584]{1,0:T(8,128)(2,1)} %bitcast.11, bf16[24,3584]{1,0:T(8,128)(2,1)} %bitcast.17, s32[1,104]{1,0:T(1,128)} %alternate_ref.1, ...), custom_call_target="tpu_custom_call" | custom-call | flops 1335885824 | bytes 4472832 | tf_op jit(solution)/shard_map/relay_tick/pallas_call | solution.py:651
  88.9 1.5 %write_out.1 = (bf16[104,3584]{1,0:T(8,128)(2,1)}, bf16[104,3584]{1,0:T(8,128)(2,1)}, bf16[104,3584]{1,0:T(8,128)(2,1)}, bf16[16,3584]{1,0:T(8,128)(2,1)}, bf16[16,3584]{1,0:T(8,128)(2,1)}) custom-call(bf16[104,3584]{1,0:T(8,128)(2,1)S(1)} %get-tuple-element.15.refs_0_, bf16[104,3584]{1,0:T(8,128)(2,1)S(1)} %get-tuple-element.16.refs_1_, ...), custom_call_target="tpu_custom_call" | custom-call | tf_op jit(solution)/shard_map/write_out/pallas_call | solution.py:719

commit v7 on v6

--- a/solution.py
+++ b/solution.py
@@ -49,7 +49,7 @@
     pre_out, pre_in, bwd_pre, act, slope_act, act_ts, grad_t, grads, by_right, by_left,
     hand, stop, opp_up, opp_dn, from_up, from_dn, opp2_up, opp2_dn, from2_up, from2_dn, sums,
     u_parts, u_opp_up, u_opp_dn, u_from_up, u_from_dn, ready,
-    local_sem, g_send, g_recv, r_send, r_recv, m_send, m_recv, y_send, y_recv, x_send, x_recv,
+    local_sem, g_send, g_recv, r_send, r_recv, m_send, m_recv, y_send, y_recv, x_send, x_recv, y_go, xz_go,
 ):
     section = lax.axis_index("section")
     dp = lax.axis_index("dp")
@@ -92,20 +92,14 @@
         pltpu.make_async_copy(wd_ref, weights.at[0, x, z], local_sem.at[4]),
         pltpu.make_async_copy(wu_ref, weights.at[1, x, z], local_sem.at[5]),
     ]
-    for load in loads:
-        load.start()
-
     y, core = lax.div(section, 2), lax.rem(section, 2)
     turn = lax.rem(y, 4)
     near = jnp.logical_or(turn == 0, turn == 3)
     far = jnp.logical_not(near)
     detours, stops, ends = turn == 2, turn == 0, turn == 1
     next_chip = {"section": lax.rem(section + 2, 16)}
-    last_chip = {"section": lax.rem(section + 14, 16)}
     stop_at = {"section": lax.rem(section + 12, 16)}
-    stop_from = {"section": lax.rem(section + 4, 16)}
     stop_to = {"section": lax.rem(y + 5, 8) * 2 + 1 - core}
-    end_from = {"section": lax.rem(y + 3, 8) * 2 + 1 - core}
 
     barrier = pltpu.get_barrier_semaphore()
 
@@ -113,13 +107,27 @@
         for partner in partners:
             pl.semaphore_signal(barrier, inc=1, device_id=partner, device_id_type=MESH)
 
-    greet(mirror, following, preceding, other, right, left, opposite, plus, minus)
-    pl.when(detours)(lambda: greet(stop_at))
-    pl.when(stops)(lambda: greet(stop_from, stop_to))
-    pl.when(ends)(lambda: greet(end_from))
-    pl.when(core == 0)(lambda: greet(next_chip, last_chip))
+    def chip_y(value):
+        return {"section": 2 * lax.rem(value + 8, 8)}
+
+    mate = {"section": section + 1 - 2 * core}
+    greet(mate, chip_y(7 - y), chip_y(y + 1), chip_y(y - 1))
+    pl.when(detours)(lambda: greet(chip_y(y - 2)))
+    pl.when(stops)(lambda: greet(chip_y(y + 2), chip_y(y + 5)))
+    pl.when(ends)(lambda: greet(chip_y(y + 3)))
+    greet(*({**to, "section": 2 * y + 1} for to in (right, left, opposite, plus, minus, other)))
+    for load in loads:
+        load.start()
     extra = jnp.where(stops, 2, jnp.where(turn == 3, 0, 1))
-    pl.semaphore_wait(barrier, 9 + extra + 2 * (1 - core))
+
+    @pl.when(core == 0)
+    def _():
+        pl.semaphore_wait(barrier, 7 + 2 * extra)
+        pl.semaphore_signal(y_go, inc=1, device_id=mate, device_id_type=MESH)
+
+    @pl.when(core == 1)
+    def _():
+        pl.semaphore_wait(y_go, 1)
 
     def piece(i):
         return pl.ds(i * PIECE, PIECE)
@@ -134,6 +142,15 @@
     shift_copies = [y_piece(out, o_section, 2 * PIECES + i, i, following) for i in range(PIECES)]
     for copy in parked_copies:
         go(copy)
+
+    @pl.when(core == 1)
+    def _():
+        pl.semaphore_wait(barrier, 13)
+        pl.semaphore_signal(xz_go, inc=1, device_id=mate, device_id_type=MESH)
+
+    @pl.when(core == 0)
+    def _():
+        pl.semaphore_wait(xz_go, 1)
 
     def send_forward(pieces, when):
         @pl.when(when)
@@ -260,22 +277,7 @@
             chosen = lax.dot_general(chosen_t, vis[:, cols], TN, preferred_element_type=F32)
             fwd[:, cols] = jnp.where(hit > 0.5, chosen, sec[:, cols].astype(F32)).astype(BF16)
         pl.when(detours)(detour_in.start)
-
-        def backward_rows():
-            total = jnp.zeros((ROWS, R), F32)
-            for i in range(PIECES):
-                parked_copies[i].wait_recv()
-                send_forward([i], near)
-                cols = piece(i)
-                total += lax.dot_general(
-                    bwd[:, cols], weight(0, cols), NT, preferred_element_type=F32
-                )
-            send_partial(2, total)
-
-            @pl.when(stops)
-            def _():
-                detour_in.wait_recv()
-                detour_out.start()
+        send_forward(range(PIECES), near)
 
     def quarter(k, first=0, size=PIECE):
         return pl.ds(pl.multiple_of(at(x + k, NX) * PIECE + first, 128), size)
@@ -332,7 +334,6 @@
         total = jnp.zeros((ROWS, R), F32)
         for i in range(PIECES):
             parked_copies[i].wait_recv()
-            send_forward([i], near)
             cols = piece(i)
             total += lax.dot_general(
                 bwd[:, cols], weight(0, cols), NT, preferred_element_type=F32
@@ -701,6 +702,8 @@
             dma((4 * PIECES,)),
             dma((9,)),
             dma((9,)),
+            pltpu.SemaphoreType.REGULAR,
+            pltpu.SemaphoreType.REGULAR,
         ],
         compiler_params=pltpu.CompilerParams(
             collective_id=0, has_side_effects=True, vmem_limit_bytes=40 * 2**20

time: 90.5 us -> 86.2 us (0.952)
  the two profiles are of different devices: /device:TPU:9 before, /device:TPU:8 now
where the time goes in v7:
time: 86.2 us; the launch traced here: 86.1 us
  Pallas kernels  85.4 us (99%)
    pallas_call x1, Pallas kernels, local(): pl.pallas_call(kernel, out_shape=(pltpu.VMEM((ROWS, D), BF16),) * 3 + (pl...  84 us

profile of v7, /device:TPU:8, one launch (start us, length us, event | category | flops | bytes accessed | tf_op | source)
XLA Modules:
  0.0 86.1 jit_solution(3835542984175699061)
XLA Ops:
  0.6 84.0 %relay_tick.1 = (bf16[104,3584]{1,0:T(8,128)(2,1)S(1)}, bf16[104,3584]{1,0:T(8,128)(2,1)S(1)}, bf16[104,3584]{1,0:T(8,128)(2,1)S(1)}, bf16[16,3584]{1,0:T(8,128)(2,1)S(1)}, bf16[16,3584]{1,0:T(8,128)(2,1)S(1)}) custom-call(bf16[104,3584]{1,0:T(8,128)(2,1)} %bitcast.11, bf16[24,3584]{1,0:T(8,128)(2,1)} %bitcast.17, s32[1,104]{1,0:T(1,128)} %alternate_ref.1, ...), custom_call_target="tpu_custom_call" | custom-call | flops 1335885824 | bytes 4472832 | tf_op jit(solution)/shard_map/relay_tick/pallas_call | solution.py:652
  84.6 1.5 %write_out.1 = (bf16[104,3584]{1,0:T(8,128)(2,1)}, bf16[104,3584]{1,0:T(8,128)(2,1)}, bf16[104,3584]{1,0:T(8,128)(2,1)}, bf16[16,3584]{1,0:T(8,128)(2,1)}, bf16[16,3584]{1,0:T(8,128)(2,1)}) custom-call(bf16[104,3584]{1,0:T(8,128)(2,1)S(1)} %get-tuple-element.15.refs_0_, bf16[104,3584]{1,0:T(8,128)(2,1)S(1)} %get-tuple-element.16.refs_1_, ...), custom_call_target="tpu_custom_call" | custom-call | tf_op jit(solution)/shard_map/write_out/pallas_call | solution.py:722

commit v8 on v7

--- a/solution.py
+++ b/solution.py
@@ -382,7 +382,7 @@
             self.a, self.b = (x, z) if x_first else (z, x)
             xs, zs = (right, left), (plus, minus)
             (self.up, self.dn), (self.up2, self.dn2) = (xs, zs) if x_first else (zs, xs)
-            middle = (start + stop) // 2
+            middle = start + (stop - start + 128) // 256 * 128
             self.all = pl.ds(start, stop - start)
             self.low, self.high = pl.ds(start, middle - start), pl.ds(middle, stop - middle)
 
@@ -420,10 +420,9 @@
             return remote(src, dst, r_send.at[index], r_recv.at[index], to)
 
         def send_far(self):
-            steps = -(-(self.stop - self.start) // 640)
-            width = (self.stop - self.start) // steps
-            for i in range(steps):
-                cols = pl.ds(self.start + i * width, width)
+            for first in range(self.start, self.stop, 640):
+                width = min(640, self.stop - first)
+                cols = pl.ds(first, width)
                 product = jnp.dot(grad_t[...], bwd[:, cols], preferred_element_type=F32)
                 parts[:, :, :, cols] = product.astype(BF16).reshape(NX, NZ, SHARE, width)
             go(self.copy(0))
@@ -478,25 +477,24 @@
 
     class ReduceUp(Reduce):
         def send_far(self):
-            for cols in (lows, highs):
-                product = jnp.zeros((R, cols.size), F32)
-                for i in range(NX):
-                    product += jnp.dot(
-                        act_ts[i], grads[i, :, cols], preferred_element_type=F32
-                    )
-                u_parts[:, :, :, cols] = product.astype(BF16).reshape(NX, NZ, SHARE, cols.size)
+            cols = self.all
+            product = jnp.zeros((R, cols.size), F32)
+            for i in range(NX):
+                product += jnp.dot(act_ts[i], grads[i, :, cols], preferred_element_type=F32)
+            u_parts[:, :, :, cols] = product.astype(BF16).reshape(NX, NZ, SHARE, cols.size)
             go(self.copy(0))
             go(self.copy(1))
 
         def owner(self, m):
             k, to = ((1, right), (-1, left), (2, opposite))[m]
-            return self.message(6 + m, ready.at[at(x + k, NX)], o_up.at[:, quarter(0)], to)
+            place = o_up.at[:, quarter(0, self.start, self.stop - self.start)]
+            return self.message(6 + m, ready.at[at(x + k, NX), :, self.all], place, to)
 
         def fold(self):
-            ready[...] = (self.folded() * (1.0 / 16)).astype(BF16)
+            ready[:, :, self.all] = (self.folded() * (1.0 / 16)).astype(BF16)
             for m in (2, 0, 1):
                 go(self.owner(m))
-            o_up[:, quarter(0)] = ready[x]
+            o_up[:, quarter(0, self.start, self.stop - self.start)] = ready[x, :, self.all]
 
         def finish(self):
             for m in range(3):
@@ -509,13 +507,16 @@
 
     down_place = (parts, opp_up, opp_dn, from_up, from_dn)
     up_place = (u_parts, u_opp_up, u_opp_dn, u_from_up, u_from_dn)
-    d0, d1 = Reduce(0, down_place, 512, 2048, True), Reduce(1, down_place, 2048, D, True)
-    dz = Reduce(2, down_place, 0, 512, False)
-    u0 = ReduceUp(3, up_place, 0, PIECE, False)
-
+    dz = Reduce(0, down_place, 0, 640, False)
+    d0 = Reduce(1, down_place, 640, 1664, True)
+    d1 = Reduce(2, down_place, 1664, 2688, True)
+    d2 = Reduce(3, down_place, 2688, 3584, True)
+    u0 = ReduceUp(4, up_place, 0, 512, False)
+    u1 = ReduceUp(5, up_place, 512, 896, False)
+
+    down.start1()
+    down.start2(0)
     both.start1()
-    down.start2(0)
-    down.start1()
     up.start2(0)
     both.start2(0)
     up.start1()
@@ -523,104 +524,118 @@
     rows_far()
     rows_near()
     choose_rows()
+    down.near2(0, 1)
+    down.near2(0, 0)
     both.near1(0)
+    down.near1(0)
+    down.near1(1)
     both.near1(1)
-    down.near2(0, 0)
-    down.near2(0, 1)
     up.near2(0, 0)
     up.near2(0, 1)
-    rows_relay(1)
-    both.far1()
     both.near2(0, 0)
     both.near2(0, 1)
+    rows_relay(1)
     rows_relay(0)
-    down.near1(0)
-    down.near1(1)
+    up.near1(0)
     up.near1(1)
-    up.near1(0)
+    down.near2(3, 1)
+    both.near2(3, 0)
+    both.near2(3, 1)
     down.far2(0)
-    down.near2(3, 1)
+    down.near2(1, 1)
+    down.far1()
+    both.far1()
+    down.near2(3, 0)
+    both.near2(1, 0)
+    both.near2(1, 1)
+    down.near2(1, 0)
+    up.near2(3, 1)
     up.far2(0)
-    down.near2(1, 1)
-    both.near2(3, 1)
-    both.near2(1, 1)
+    both.far2(0)
     up.near2(1, 1)
-    up.near2(3, 1)
-    both.near2(3, 0)
-    both.near2(1, 0)
+    rows_done()
+    up.far1()
+    both.far2(3)
+    down.far2(3)
+    up.near2(3, 0)
+    down.far2(1)
+    both.near2(2, 0)
     both.near2(2, 1)
-    down.far1()
-    down.near2(3, 0)
-    down.near2(1, 0)
-    up.far1()
-    rows_done()
     up.near2(1, 0)
-    up.near2(3, 0)
-    both.near2(2, 0)
-    both.far2(0)
-    down.far2(3)
-    down.far2(1)
+    down.near2(2, 1)
     down.near2(2, 0)
-    both.far2(3)
+    up.far2(3)
     both.far2(1)
     up.near2(2, 0)
     both.far2(2)
     up.far2(1)
-    up.far2(3)
-    down.near2(2, 1)
+    down.far2(2)
+    partial(0, fwd, 0)
     up.near2(2, 1)
-    down.far2(2)
+    up.far2(2)
     backward_rows()
-    partial(0, fwd, 0)
-    up.far2(2)
     partial(1, grad, 1)
-    backward_act()
-    act_send()
     act[...] = gelu(summed(0)).astype(BF16)
     outputs(0)
     outputs(1)
+    backward_act()
+    act_send()
     outputs(2)
     slopes()
+    d1.send_far()
     dz.send_far()
     act_relay()
+    d0.send_far()
     dz.send_near()
-    d0.send_far()
-    d1.send_far()
+    d1.send_near()
     d0.send_near()
-    d1.send_near()
+    d2.send_far()
+    d1.relay(1)
+    d1.relay(0)
+    d2.send_near()
     outputs(3)
     send_forward(range(last), far)
     send_forward([last], ends)
+    dz.relay(0)
+    dz.relay(1)
+    d0.relay(0)
     act_done()
     u0.send_far()
-    dz.relay(1)
-    dz.relay(0)
+    d0.relay(1)
+    u1.send_far()
     u0.send_near()
+    dz.fold()
+    d2.relay(0)
+    u1.send_near()
     input_grad(0)
-    input_grad(1)
-    pass_on()
-    input_grad(2)
-    d0.relay(0)
-    input_grad(3)
-    d0.relay(1)
-    d1.relay(1)
-    d1.relay(0)
-    dz.fold()
     u0.relay(0)
     u0.relay(1)
+    d2.relay(1)
+    input_grad(1)
+    u1.relay(0)
+    u1.relay(1)
+    input_grad(2)
+    pass_on()
+    d1.fold()
+    input_grad(3)
+    dz.relay2(0)
     d0.fold()
-    dz.relay2(0)
     dz.relay2(1)
-    d1.fold()
+    u0.fold()
+    u1.fold()
+    d2.fold()
+    d1.relay2(1)
+    d1.relay2(0)
     dz.finish()
     d0.relay2(0)
     d0.relay2(1)
-    u0.fold()
-    d1.relay2(0)
-    d1.relay2(1)
+    u0.finish()
+    u1.finish()
+    d2.relay2(0)
+    d2.relay2(1)
+    d1.finish()
     d0.finish()
-    u0.finish()
-    d1.finish()
+    d2.finish()
 
     for copy in forward_copies + shift_copies:
         copy.wait_recv()
@@ -694,8 +709,8 @@
             dma((6,)),
             dma((3 * N_GATHER,)),
             dma((3 * N_GATHER,)),
-            dma((4 * N_REDUCE,)),
-            dma((4 * N_REDUCE,)),
+            dma((6 * N_REDUCE,)),
+            dma((6 * N_REDUCE,)),
             dma((3,)),
             dma((3,)),
             dma((4 * PIECES,)),

time: 86.2 us -> 87.8 us (1.019)
  the two profiles are of different devices: /device:TPU:8 before, /device:TPU:24 now
where the time goes in v8:
time: 87.8 us; the launch traced here: 87.7 us
  Pallas kernels  87.1 us (99%)
    pallas_call x1, Pallas kernels, local(): pl.pallas_call(kernel, out_shape=(pltpu.VMEM((ROWS, D), BF16),) * 3 + (pl...  85.6 us

profile of v8, /device:TPU:24, one launch (start us, length us, event | category | flops | bytes accessed | tf_op | source)
XLA Modules:
  0.0 87.7 jit_solution(9178278591959903143)
XLA Ops:
  0.6 85.6 %relay_tick.1 = (bf16[104,3584]{1,0:T(8,128)(2,1)S(1)}, bf16[104,3584]{1,0:T(8,128)(2,1)S(1)}, bf16[104,3584]{1,0:T(8,128)(2,1)S(1)}, bf16[16,3584]{1,0:T(8,128)(2,1)S(1)}, bf16[16,3584]{1,0:T(8,128)(2,1)S(1)}) custom-call(bf16[104,3584]{1,0:T(8,128)(2,1)} %bitcast.11, bf16[24,3584]{1,0:T(8,128)(2,1)} %bitcast.17, s32[1,104]{1,0:T(1,128)} %alternate_ref.1, ...), custom_call_target="tpu_custom_call" | custom-call | flops 1335885824 | bytes 4472832 | tf_op jit(solution)/shard_map/relay_tick/pallas_call | solution.py:667
  86.2 1.5 %write_out.1 = (bf16[104,3584]{1,0:T(8,128)(2,1)}, bf16[104,3584]{1,0:T(8,128)(2,1)}, bf16[104,3584]{1,0:T(8,128)(2,1)}, bf16[16,3584]{1,0:T(8,128)(2,1)}, bf16[16,3584]{1,0:T(8,128)(2,1)}) custom-call(bf16[104,3584]{1,0:T(8,128)(2,1)S(1)} %get-tuple-element.15.refs_0_, bf16[104,3584]{1,0:T(8,128)(2,1)S(1)} %get-tuple-element.16.refs_1_, ...), custom_call_target="tpu_custom_call" | custom-call | tf_op jit(solution)/shard_map/write_out/pallas_call | solution.py:737

commit v9 on v8

--- a/solution.py
+++ b/solution.py
@@ -22,7 +22,7 @@
 HANDED = 2
 HAND = 3 * PIECES
 NX, NZ = 4, 4
-SPLIT = 1024
+SPLIT = 768
 
 N_GATHER = 16
 N_REDUCE = 12
@@ -507,135 +507,117 @@
 
     down_place = (parts, opp_up, opp_dn, from_up, from_dn)
     up_place = (u_parts, u_opp_up, u_opp_dn, u_from_up, u_from_dn)
-    dz = Reduce(0, down_place, 0, 640, False)
-    d0 = Reduce(1, down_place, 640, 1664, True)
-    d1 = Reduce(2, down_place, 1664, 2688, True)
-    d2 = Reduce(3, down_place, 2688, 3584, True)
-    u0 = ReduceUp(4, up_place, 0, 512, False)
-    u1 = ReduceUp(5, up_place, 512, 896, False)
-
+    dz = Reduce(0, down_place, 0, 768, False)
+    d0 = Reduce(1, down_place, 768, 3584, True)
+    u0 = ReduceUp(2, up_place, 0, 512, False)
+    u1 = ReduceUp(3, up_place, 512, 896, False)
+
+    both.start1()
+    up.start1()
+    up.start2(0)
     down.start1()
+    both.start2(0)
     down.start2(0)
-    both.start1()
-    up.start2(0)
-    both.start2(0)
-    up.start1()
     loads[3].wait()
     rows_far()
     rows_near()
     choose_rows()
-    down.near2(0, 1)
-    down.near2(0, 0)
-    both.near1(0)
+    up.near1(0)
+    up.near1(1)
     down.near1(0)
     down.near1(1)
     both.near1(1)
+    both.near2(0, 0)
+    both.near1(0)
+    up.near2(0, 1)
+    both.near2(0, 1)
+    up.far1()
     up.near2(0, 0)
-    up.near2(0, 1)
-    both.near2(0, 0)
-    both.near2(0, 1)
+    down.near2(0, 1)
+    down.far1()
+    down.near2(0, 0)
     rows_relay(1)
-    rows_relay(0)
-    up.near1(0)
-    up.near1(1)
-    down.near2(3, 1)
-    both.near2(3, 0)
-    both.near2(3, 1)
-    down.far2(0)
-    down.near2(1, 1)
-    down.far1()
-    both.far1()
-    down.near2(3, 0)
     both.near2(1, 0)
     both.near2(1, 1)
+    rows_relay(0)
+    both.far2(0)
+    both.near2(3, 1)
+    both.near2(3, 0)
+    both.far2(1)
+    up.near2(3, 1)
+    up.near2(3, 0)
+    up.near2(1, 1)
+    both.far2(3)
+    up.near2(1, 0)
+    down.near2(3, 1)
+    down.near2(3, 0)
+    down.near2(1, 1)
     down.near2(1, 0)
-    up.near2(3, 1)
+    both.far1()
+    up.near2(2, 1)
+    up.near2(2, 0)
+    down.near2(2, 1)
     up.far2(0)
-    both.far2(0)
-    up.near2(1, 1)
-    rows_done()
-    up.far1()
-    both.far2(3)
-    down.far2(3)
-    up.near2(3, 0)
-    down.far2(1)
     both.near2(2, 0)
     both.near2(2, 1)
-    up.near2(1, 0)
-    down.near2(2, 1)
     down.near2(2, 0)
     up.far2(3)
-    both.far2(1)
-    up.near2(2, 0)
+    down.far2(0)
+    up.far2(1)
     both.far2(2)
-    up.far2(1)
+    rows_done()
+    down.far2(3)
+    up.far2(2)
+    partial(1, grad, 1)
+    down.far2(1)
     down.far2(2)
+    backward_rows()
     partial(0, fwd, 0)
-    up.near2(2, 1)
-    up.far2(2)
-    backward_rows()
-    partial(1, grad, 1)
+    backward_act()
+    act_send()
+    slopes()
+    dz.send_far()
+    d0.send_far()
+    d0.send_near()
+    dz.send_near()
+    dz.relay(0)
+    dz.relay(1)
     act[...] = gelu(summed(0)).astype(BF16)
     outputs(0)
     outputs(1)
-    backward_act()
-    act_send()
     outputs(2)
-    slopes()
-    d1.send_far()
-    dz.send_far()
     act_relay()
-    d0.send_far()
-    dz.send_near()
-    d1.send_near()
-    d0.send_near()
-    d2.send_far()
-    d1.relay(1)
-    d1.relay(0)
-    d2.send_near()
     outputs(3)
     send_forward(range(last), far)
     send_forward([last], ends)
-    dz.relay(0)
-    dz.relay(1)
     d0.relay(0)
+    input_grad(0)
+    input_grad(1)
+    d0.relay(1)
+    input_grad(2)
+    pass_on()
+    input_grad(3)
     act_done()
     u0.send_far()
-    d0.relay(1)
+    u0.send_near()
     u1.send_far()
-    u0.send_near()
+    d0.fold()
     dz.fold()
-    d2.relay(0)
+    u0.relay(1)
+    u0.relay(0)
     u1.send_near()
-    input_grad(0)
-    u0.relay(0)
-    u0.relay(1)
-    d2.relay(1)
-    input_grad(1)
     u1.relay(0)
     u1.relay(1)
-    input_grad(2)
-    pass_on()
-    d1.fold()
-    input_grad(3)
+    dz.relay2(1)
     dz.relay2(0)
-    d0.fold()
-    dz.relay2(1)
-    u0.fold()
-    u1.fold()
-    d2.fold()
-    d1.relay2(1)
-    d1.relay2(0)
-    dz.finish()
     d0.relay2(0)
     d0.relay2(1)
+    u0.fold()
+    dz.finish()
+    u1.fold()
+    d0.finish()
     u0.finish()
     u1.finish()
-    d2.relay2(0)
-    d2.relay2(1)
-    d1.finish()
-    d0.finish()
-    d2.finish()
 
     for copy in forward_copies + shift_copies:
         copy.wait_recv()
@@ -709,8 +691,8 @@
             dma((6,)),
             dma((3 * N_GATHER,)),
             dma((3 * N_GATHER,)),
-            dma((6 * N_REDUCE,)),
-            dma((6 * N_REDUCE,)),
+            dma((4 * N_REDUCE,)),
+            dma((4 * N_REDUCE,)),
             dma((3,)),
             dma((3,)),
             dma((4 * PIECES,)),

time: 87.8 us -> 89.9 us (1.024)
  the two profiles are of different devices: /device:TPU:24 before, /device:TPU:6 now
where the time goes in v9:
time: 89.9 us; the launch traced here: 89.8 us
  Pallas kernels  89.2 us (99%)
    pallas_call x1, Pallas kernels, local(): pl.pallas_call(kernel, out_shape=(pltpu.VMEM((ROWS, D), BF16),) * 3 + (pl...  87.7 us

profile of v9, /device:TPU:6, one launch (start us, length us, event | category | flops | bytes accessed | tf_op | source)
XLA Modules:
  0.0 89.8 jit_solution(11652386643751626586)
XLA Ops:
  0.6 87.7 %relay_tick.1 = (bf16[104,3584]{1,0:T(8,128)(2,1)S(1)}, bf16[104,3584]{1,0:T(8,128)(2,1)S(1)}, bf16[104,3584]{1,0:T(8,128)(2,1)S(1)}, bf16[16,3584]{1,0:T(8,128)(2,1)S(1)}, bf16[16,3584]{1,0:T(8,128)(2,1)S(1)}) custom-call(bf16[104,3584]{1,0:T(8,128)(2,1)} %bitcast.11, bf16[24,3584]{1,0:T(8,128)(2,1)} %bitcast.17, s32[1,104]{1,0:T(1,128)} %alternate_ref.1, ...), custom_call_target="tpu_custom_call" | custom-call | flops 1335885824 | bytes 4472832 | tf_op jit(solution)/shard_map/relay_tick/pallas_call | solution.py:649
  88.4 1.5 %write_out.1 = (bf16[104,3584]{1,0:T(8,128)(2,1)}, bf16[104,3584]{1,0:T(8,128)(2,1)}, bf16[104,3584]{1,0:T(8,128)(2,1)}, bf16[16,3584]{1,0:T(8,128)(2,1)}, bf16[16,3584]{1,0:T(8,128)(2,1)}) custom-call(bf16[104,3584]{1,0:T(8,128)(2,1)S(1)} %get-tuple-element.15.refs_0_, bf16[104,3584]{1,0:T(8,128)(2,1)S(1)} %get-tuple-element.16.refs_1_, ...), custom_call_target="tpu_custom_call" | custom-call | tf_op jit(solution)/shard_map/write_out/pallas_call | solution.py:719

commit v10 on v7

--- a/solution.py
+++ b/solution.py
@@ -382,7 +382,7 @@
             self.a, self.b = (x, z) if x_first else (z, x)
             xs, zs = (right, left), (plus, minus)
             (self.up, self.dn), (self.up2, self.dn2) = (xs, zs) if x_first else (zs, xs)
-            middle = (start + stop) // 2
+            middle = start + (stop - start + 128) // 256 * 128
             self.all = pl.ds(start, stop - start)
             self.low, self.high = pl.ds(start, middle - start), pl.ds(middle, stop - middle)
 
@@ -420,10 +420,9 @@
             return remote(src, dst, r_send.at[index], r_recv.at[index], to)
 
         def send_far(self):
-            steps = -(-(self.stop - self.start) // 640)
-            width = (self.stop - self.start) // steps
-            for i in range(steps):
-                cols = pl.ds(self.start + i * width, width)
+            for first in range(self.start, self.stop, 640):
+                width = min(640, self.stop - first)
+                cols = pl.ds(first, width)
                 product = jnp.dot(grad_t[...], bwd[:, cols], preferred_element_type=F32)
                 parts[:, :, :, cols] = product.astype(BF16).reshape(NX, NZ, SHARE, width)
             go(self.copy(0))
@@ -478,25 +477,24 @@
 
     class ReduceUp(Reduce):
         def send_far(self):
-            for cols in (lows, highs):
-                product = jnp.zeros((R, cols.size), F32)
-                for i in range(NX):
-                    product += jnp.dot(
-                        act_ts[i], grads[i, :, cols], preferred_element_type=F32
-                    )
-                u_parts[:, :, :, cols] = product.astype(BF16).reshape(NX, NZ, SHARE, cols.size)
+            cols = self.all
+            product = jnp.zeros((R, cols.size), F32)
+            for i in range(NX):
+                product += jnp.dot(act_ts[i], grads[i, :, cols], preferred_element_type=F32)
+            u_parts[:, :, :, cols] = product.astype(BF16).reshape(NX, NZ, SHARE, cols.size)
             go(self.copy(0))
             go(self.copy(1))
 
         def owner(self, m):
             k, to = ((1, right), (-1, left), (2, opposite))[m]
-            return self.message(6 + m, ready.at[at(x + k, NX)], o_up.at[:, quarter(0)], to)
+            place = o_up.at[:, quarter(0, self.start, self.stop - self.start)]
+            return self.message(6 + m, ready.at[at(x + k, NX), :, self.all], place, to)
 
         def fold(self):
-            ready[...] = (self.folded() * (1.0 / 16)).astype(BF16)
+            ready[:, :, self.all] = (self.folded() * (1.0 / 16)).astype(BF16)
             for m in (2, 0, 1):
                 go(self.owner(m))
-            o_up[:, quarter(0)] = ready[x]
+            o_up[:, quarter(0, self.start, self.stop - self.start)] = ready[x, :, self.all]
 
         def finish(self):
             for m in range(3):
@@ -509,15 +507,17 @@
 
     down_place = (parts, opp_up, opp_dn, from_up, from_dn)
     up_place = (u_parts, u_opp_up, u_opp_dn, u_from_up, u_from_dn)
-    d0, d1 = Reduce(0, down_place, 512, 2048, True), Reduce(1, down_place, 2048, D, True)
-    dz = Reduce(2, down_place, 0, 512, False)
-    u0 = ReduceUp(3, up_place, 0, PIECE, False)
+    dz = Reduce(0, down_place, 0, 768, False)
+    d0 = Reduce(1, down_place, 768, 2176, True)
+    d1 = Reduce(2, down_place, 2176, 3584, True)
+    u0 = ReduceUp(3, up_place, 0, 384, False)
+    u1 = ReduceUp(4, up_place, 384, 896, False)
 
     both.start1()
-    down.start2(0)
     down.start1()
     up.start2(0)
     both.start2(0)
+    down.start2(0)
     up.start1()
     loads[3].wait()
     rows_far()
@@ -525,10 +525,10 @@
     choose_rows()
     both.near1(0)
     both.near1(1)
+    up.near2(0, 0)
+    up.near2(0, 1)
     down.near2(0, 0)
     down.near2(0, 1)
-    up.near2(0, 0)
-    up.near2(0, 1)
     rows_relay(1)
     both.far1()
     both.near2(0, 0)
@@ -538,10 +538,10 @@
     down.near1(1)
     up.near1(1)
     up.near1(0)
+    up.far2(0)
+    down.near2(3, 1)
+    down.near2(1, 1)
     down.far2(0)
-    down.near2(3, 1)
-    up.far2(0)
-    down.near2(1, 1)
     both.near2(3, 1)
     both.near2(1, 1)
     up.near2(1, 1)
@@ -555,8 +555,8 @@
     up.far1()
     rows_done()
     up.near2(1, 0)
+    both.near2(2, 0)
     up.near2(3, 0)
-    both.near2(2, 0)
     both.far2(0)
     down.far2(3)
     down.far2(1)
@@ -568,9 +568,9 @@
     up.far2(1)
     up.far2(3)
     down.near2(2, 1)
-    up.near2(2, 1)
     down.far2(2)
     backward_rows()
+    up.near2(2, 1)
     partial(0, fwd, 0)
     up.far2(2)
     partial(1, grad, 1)
@@ -593,33 +593,39 @@
     send_forward([last], ends)
     act_done()
     u0.send_far()
+    u0.send_near()
+    u1.send_far()
     dz.relay(1)
     dz.relay(0)
-    u0.send_near()
+    u1.send_near()
     input_grad(0)
+    d0.relay(0)
     input_grad(1)
     pass_on()
-    input_grad(2)
-    d0.relay(0)
-    input_grad(3)
     d0.relay(1)
-    d1.relay(1)
-    d1.relay(0)
-    dz.fold()
     u0.relay(0)
     u0.relay(1)
+    input_grad(2)
+    input_grad(3)
+    d1.relay(0)
+    d1.relay(1)
+    u1.relay(0)
+    u1.relay(1)
     d0.fold()
+    u0.fold()
+    dz.fold()
+    d1.fold()
+    u0.finish()
     dz.relay2(0)
     dz.relay2(1)
-    d1.fold()
-    dz.finish()
+    u1.fold()
     d0.relay2(0)
     d0.relay2(1)
-    u0.fold()
+    dz.finish()
     d1.relay2(0)
     d1.relay2(1)
+    u1.finish()
     d0.finish()
-    u0.finish()
     d1.finish()
 
     for copy in forward_copies + shift_copies:
@@ -694,8 +700,8 @@
             dma((6,)),
             dma((3 * N_GATHER,)),
             dma((3 * N_GATHER,)),
-            dma((4 * N_REDUCE,)),
-            dma((4 * N_REDUCE,)),
+            dma((5 * N_REDUCE,)),
+            dma((5 * N_REDUCE,)),
             dma((3,)),
             dma((3,)),
             dma((4 * PIECES,)),

time: 86.2 us -> 89.2 us (1.035)
  Pallas kernels: 85.4 us -> 88.5 us
    pallas_call x1, Pallas kernels: 84 us -> 87 us  [local(): pl.pallas_call(kernel, out_shape=(pltpu.VMEM((ROWS, D), BF16),) * 3 + (pl...]
where the time goes in v10:
time: 89.2 us; the launch traced here: 89.1 us
  Pallas kernels  88.5 us (99%)
    pallas_call x1, Pallas kernels, local(): pl.pallas_call(kernel, out_shape=(pltpu.VMEM((ROWS, D), BF16),) * 3 + (pl...  87 us

profile of v10, /device:TPU:8, one launch (start us, length us, event | category | flops | bytes accessed | tf_op | source)
XLA Modules:
  0.0 89.1 jit_solution(7977947202792496670)
XLA Ops:
  0.6 87.0 %relay_tick.1 = (bf16[104,3584]{1,0:T(8,128)(2,1)S(1)}, bf16[104,3584]{1,0:T(8,128)(2,1)S(1)}, bf16[104,3584]{1,0:T(8,128)(2,1)S(1)}, bf16[16,3584]{1,0:T(8,128)(2,1)S(1)}, bf16[16,3584]{1,0:T(8,128)(2,1)S(1)}) custom-call(bf16[104,3584]{1,0:T(8,128)(2,1)} %bitcast.11, bf16[24,3584]{1,0:T(8,128)(2,1)} %bitcast.17, s32[1,104]{1,0:T(1,128)} %alternate_ref.1, ...), custom_call_target="tpu_custom_call" | custom-call | flops 1335885824 | bytes 4472832 | tf_op jit(solution)/shard_map/relay_tick/pallas_call | solution.py:658
  87.7 1.5 %write_out.1 = (bf16[104,3584]{1,0:T(8,128)(2,1)}, bf16[104,3584]{1,0:T(8,128)(2,1)}, bf16[104,3584]{1,0:T(8,128)(2,1)}, bf16[16,3584]{1,0:T(8,128)(2,1)}, bf16[16,3584]{1,0:T(8,128)(2,1)}) custom-call(bf16[104,3584]{1,0:T(8,128)(2,1)S(1)} %get-tuple-element.15.refs_0_, bf16[104,3584]{1,0:T(8,128)(2,1)S(1)} %get-tuple-element.16.refs_1_, ...), custom_call_target="tpu_custom_call" | custom-call | tf_op jit(solution)/shard_map/write_out/pallas_call | solution.py:728
